TPU v7x, 32 devices: a whole 2x2x4 slice. The times are simulated.
32 devices in a mesh: parts: 2 (over x), tiles: 16 (over z, y, core).
Axes of the slice: x: 2, y: 2, z: 4, core: 2. Of those that a mesh axis runs over, the one named last changes fastest.
Arguments:
- mask_params: float32 [4096, 1024], P(('parts', 'tiles')), parts along dimension 0, may hold values from -6 to 6
- target: int32 [4096, 1024], P(('parts', 'tiles')), parts along dimension 0, may hold values 0 or 1
- kernel_spectra: float32 [2, 16, 32, 128], replicated, may hold values from -0.0625 to 0.0625
- kernel_weights: float32 [16], replicated, may hold values from 0.05 to 1
Outputs:
- resist_image: float32 [4096, 1024], P(('parts', 'tiles')), parts along dimension 0
- mask_gradient: float32 [4096, 1024], P(('parts', 'tiles')), parts along dimension 0
There are 2 independent parts, one for each index of `parts`. A program takes and returns all parts, laid end to end along the dimension named above; an argument that names none is the same for every part. Nothing has to cross between parts.
All inputs are finite; a program needn't handle non-finite values. No bound on the sum of `target` on one device may be relied on, other than what follows from the above.
Results may differ from a plain program's by a relative error of at most 0.0003.
Values sent between devices are 32-bit elements; how exact they have to be, the bound alone decides.
A program may use at most 64 MiB of HBM per device.

v0:
```python
import math

import jax
import jax.numpy as jnp
from jax import lax
from jax.sharding import PartitionSpec as P

MARGIN = 64


STEEPNESS = 8.0
THRESHOLD = 0.35
HIGHEST = lax.Precision.HIGHEST


def with_halo(block, sides, width):
    for axis, dim in sides:
        count = lax.axis_size(axis)
        forward = [(i, i + 1) for i in range(count - 1)]
        forward.append((count - 1, 0))
        backward = [(target, source) for source, target in forward]
        low = lax.ppermute(
            lax.slice_in_dim(block, block.shape[dim] - width, None, axis=dim), axis, forward
        )
        high = lax.ppermute(lax.slice_in_dim(block, 0, width, axis=dim), axis, backward)
        block = jnp.concatenate([low, block, high], axis=dim)
    return block


def matmul(left, right):
    return jnp.dot(left, right, precision=HIGHEST, preferred_element_type=jnp.float32)


def phase_table(frequencies, positions, length):
    cycles = jnp.remainder(frequencies[:, None] * positions[None, :], length).astype(jnp.float32)
    angles = cycles * (2.0 * math.pi / length)
    return (jnp.cos(angles), jnp.sin(angles))


def make_tables(strip_rows, margin, columns, freq_rows, freq_cols):
    window = strip_rows + 2 * margin
    col_freq = jnp.arange(freq_cols, dtype=jnp.int32) - freq_cols // 2
    row_freq = jnp.arange(freq_rows, dtype=jnp.int32) - freq_rows // 2
    col_cos, col_sin = phase_table(col_freq, jnp.arange(columns, dtype=jnp.int32), columns)
    row_cos, row_sin = phase_table(row_freq, jnp.arange(window, dtype=jnp.int32), window)
    factor = 1.0 / math.sqrt(window * columns)
    forward_cols = jnp.concatenate([col_cos.T, -col_sin.T], axis=1) * factor
    row_stack = jnp.concatenate([row_cos, row_sin], axis=0)
    own_rows = row_stack[:, margin : margin + strip_rows].T
    inverse_cols = jnp.concatenate(
        [jnp.concatenate([col_cos, col_sin], axis=1), jnp.concatenate([-col_sin, col_cos], axis=1)],
        axis=0,
    )
    return (forward_cols, row_stack, own_rows, inverse_cols)


def kernel_fields(window_spec, kernel_spectra, own_rows):
    half_rows = window_spec.shape[0] // 2
    half_cols = window_spec.shape[1] // 2
    spec_real = window_spec[:half_rows, :half_cols] + window_spec[half_rows:, half_cols:]
    spec_imag = window_spec[:half_rows, half_cols:] - window_spec[half_rows:, :half_cols]
    kern_real = kernel_spectra[0]
    kern_imag = kernel_spectra[1]
    prod_real = kern_real * spec_real - kern_imag * spec_imag
    prod_imag = kern_real * spec_imag + kern_imag * spec_real
    blocked = jnp.concatenate(
        [
            jnp.concatenate([prod_real, prod_imag], axis=2),
            jnp.concatenate([-prod_imag, prod_real], axis=2),
        ],
        axis=1,
    )
    return jnp.einsum("pr,krc->kpc", own_rows, blocked, precision=HIGHEST)


def window_adjoint(inner_grad, kernel_spectra, own_rows):
    half_rows = own_rows.shape[1] // 2
    half_cols = inner_grad.shape[2] // 2
    spec_grad = jnp.einsum("pr,kpc->krc", own_rows, inner_grad, precision=HIGHEST)
    grad_real = spec_grad[:, :half_rows, :half_cols] + spec_grad[:, half_rows:, half_cols:]
    grad_imag = spec_grad[:, :half_rows, half_cols:] - spec_grad[:, half_rows:, :half_cols]
    kern_real = kernel_spectra[0]
    kern_imag = kernel_spectra[1]
    win_real = jnp.sum(grad_real * kern_real + grad_imag * kern_imag, axis=0)
    win_imag = jnp.sum(grad_imag * kern_real - grad_real * kern_imag, axis=0)
    return jnp.concatenate(
        [
            jnp.concatenate([win_real, win_imag], axis=1),
            jnp.concatenate([-win_imag, win_real], axis=1),
        ],
        axis=0,
    )


def shards(mask_params, target, kernel_spectra, kernel_weights):
    strip_rows, columns = mask_params.shape
    margin = MARGIN
    freq_rows = kernel_spectra.shape[2]
    freq_cols = kernel_spectra.shape[3]
    kernels = kernel_spectra.shape[1]
    forward_cols, row_stack, own_rows, inverse_cols = make_tables(
        strip_rows, margin, columns, freq_rows, freq_cols
    )
    transmit = jnp.tanh(mask_params)
    padded = with_halo(transmit, (("tiles", 0),), margin)
    window_spec = matmul(row_stack, matmul(padded, forward_cols))
    inner = kernel_fields(window_spec, kernel_spectra, own_rows)
    blocks = kernels // 4
    shares = kernel_weights / jnp.sum(kernel_weights)
    inner_blocks = inner.reshape(blocks, 4, strip_rows, 2 * freq_cols)
    share_blocks = shares.reshape(blocks, 4)

    def add_power(totals, items):
        inner_block, share_block = items
        fields = jnp.einsum("kpc,cw->kpw", inner_block, inverse_cols, precision=HIGHEST)
        powers = fields[:, :, :columns] ** 2 + fields[:, :, columns:] ** 2
        return (totals + jnp.einsum("k,kpw->pw", share_block, powers, precision=HIGHEST), fields)

    intensity, field_blocks = lax.scan(
        add_power, jnp.zeros((strip_rows, columns), jnp.float32), (inner_blocks, share_blocks)
    )
    resist = jax.nn.sigmoid(STEEPNESS * (intensity - THRESHOLD))
    slopes = 2.0 * (resist - target.astype(jnp.float32)) * STEEPNESS * resist * (1.0 - resist)
    doubled = jnp.concatenate([slopes, slopes], axis=1)

    def adjoint_block(running, items):
        fields, share_block = items
        field_grad = (2.0 * share_block)[:, None, None] * doubled[None] * fields
        return (running, jnp.einsum("kpw,cw->kpc", field_grad, inverse_cols, precision=HIGHEST))

    _, inner_grad = lax.scan(
        adjoint_block, jnp.zeros((), jnp.float32), (field_blocks, share_blocks)
    )
    inner_grad = inner_grad.reshape(kernels, strip_rows, 2 * freq_cols)
    window_grad = window_adjoint(inner_grad, kernel_spectra, own_rows)
    framed_grad = with_halo(window_grad[None], (("tiles", 0),), 1)
    merged_grad = matmul(row_stack[:, margin : margin + strip_rows].T, window_grad)
    merged_grad = merged_grad.at[:margin].add(
        matmul(row_stack[:, margin + strip_rows :].T, framed_grad[0])
    )
    merged_grad = merged_grad.at[strip_rows - margin :].add(
        matmul(row_stack[:, :margin].T, framed_grad[2])
    )
    mask_grad = matmul(merged_grad, forward_cols.T)
    gradient = mask_grad * (1.0 - transmit * transmit)
    return (resist, gradient)


def solution(mesh):
    in_specs = (P(("parts", "tiles"), None), P(("parts", "tiles"), None), P(), P())
    out_specs = (P(("parts", "tiles"), None), P(("parts", "tiles"), None))
    return jax.shard_map(shards, mesh=mesh, in_specs=in_specs, out_specs=out_specs, check_vma=False)
```

profile of v0, /device:TPU:0, one launch (start us, length us, event | category | flops | bytes accessed | tf_op | source)
XLA Modules:
  0.0 110.2 jit_solution(16681351055351591656)
XLA Ops:
  0.6 1.1 %tanh.3 = f32[128,1024]{1,0:T(8,128)S(1)} tanh(f32[128,1024]{1,0:T(8,128)} %param.12) | non-fusion elementwise | bytes 1048576 | tf_op jit(solution)/shard_map/tanh | solution.py:104
  1.8 0.8 fusion.99
  3.1 5.0 %collective-permute-start.1 = (f32[64,1024]{1,0:T(8,128)S(1)}, f32[64,1024]{1,0:T(8,128)}, u32[]{:S(2)}, u32[]{:S(2)}) collective-permute-start(f32[64,1024]{1,0:T(8,128)S(1)} %get-tuple-element.155), channel_id=1, source_target_pairs={{1,0},{2,1},{3,2},{4,3},{5,4},{6,5},{7,6},{8,7},{9,8},{10,9},{11,1... | collective-permute-start | bytes 786440 | tf_op jit(solution)/shard_map/ppermute | solution.py:25
  8.3 3.1 %fusion.61 = (f32[128,1024]{1,0:T(8,128)S(1)}, f32[128,1024]{1,0:T(8,128)S(1)}, f32[128,1024]{1,0:T(8,128)}) fusion(s32[128]{0:T(128)S(1)} %iota_add_fusion), kind=kLoop, calls=%fused_computation.89 | loop fusion | flops 1966080 | bytes 1573376 | tf_op jit(solution)/shard_map/sin | solution.py:37
  11.4 0.7 reduce_sum.27
  12.1 1.4 %maximum_maximum_fusion = f32[256,2048]{1,0:T(8,128)S(1)} fusion(f32[128,1024]{1,0:T(8,128)} %get-tuple-element.160, f32[128,1024]{1,0:T(8,128)S(1)} %get-tuple-element.159, f32[128,1024]{1,0:T(8,128)S(1)} %get-tuple-element.158), kind=kLoop, calls=%fused_computation.27 | loop fusion | flops 1572864 | bytes 3670016 | tf_op jit(solution)/shard_map/concatenate | solution.py:50
  14.2 2.1 %fusion.63 = (f32[1024,128]{1,0:T(8,128)S(1)}, f32[1024,128]{1,0:T(8,128)S(1)}) fusion(s32[128]{0:T(128)S(1)} %iota_add_fusion), kind=kLoop, calls=%fused_computation.91 | loop fusion | flops 1966080 | bytes 1049088 | tf_op jit(solution)/shard_map/cos | solution.py:37
  16.3 2.6 %fusion.27 = f32[256,256]{1,0:T(8,128)S(1)} fusion(f32[64,1024]{1,0:T(8,128)} %collective-permute-done.1, f32[128,1024]{1,0:T(8,128)} %copy-done.7, f32[64,1024]{1,0:T(8,128)} %collective-permute-done, f32[1024,128]{1,0:T(8,128)S(1)} %get-tuple-element.164, f32[1024,128]{1,0:T(8,128)S(1)} %get-tuple-element.163), kind=kOutput, calls=%fused_computation.34 | convolution fusion | flops 806354944 | bytes 2359296 | tf_op jit(solution)/shard_map/dot_general | solution.py:31
  19.3 4.8 %fusion.33 = f32[16,256,128]{2,1,0:T(8,128)} fusion(f32[16,32,128]{2,1,0:T(8,128)S(1)} %get-tuple-element.153, f32[16,32,128]{2,1,0:T(8,128)S(1)} %get-tuple-element.149, f32[16,32,128]{2,1,0:T(8,128)S(1)} %get-tuple-element.150, f32[32,256]{1,0:T(8,128)S(1)} %get-tuple-element.161, f32[32,256]{1,0:T(8,128)S(1)} %get-tuple-element.162), kind=kOutput, calls=%fused_computation.41 | convolution fusion | flops 403447808 | bytes 2949120 | tf_op jit(solution)/shard_map/pr,krc->kpc/dot_general | solution.py:73
  24.1 45.1 %while.26 = (s32[]{:T(128)}, f32[128,1024]{1,0:T(8,128)S(1)}, f32[4,4,128,2048]{3,2,1,0:T(8,128)}, f32[4,4]{1,0:T(4,128)S(1)}, f32[4,4,128,256]{2,3,1,0:T(8,128)...) while((s32[]{:T(128)}, f32[128,1024]{1,0:T(8,128)S(1)}, f32[4,4,128,2048]{3,2,1,0:T(8,128)}, ...), condition=%wide.region_2.3_spmd.clone, body=%wide.region_1.2_spmd.clone.sunk | while | flops 3229351936 | bytes 21497440 | solution.py:119
  24.1 6.1 %bitcast_dynamic-update-slice_fusion.2 = (f32[4,4,128,2048]{3,2,1,0:T(8,128)}, f32[4,128,2048]{2,1,0:T(8,128)S(1)}) fusion(f32[4,4,128,2048]{3,2,1,0:T(8,128)} %get-tuple-element.253, s32[]{:T(128)} %get-tuple-element.251, f32[256,2048]{1,0:T(8,128)S(1)} %get-tuple-element.264, f32[4,4,128,256]{2,3,1,0:T(8,128)} %get-tuple-element.263), kind=kOutput, calls=%fused_computation.13.clone.1 | convolution fusion | flops 3221225472 | bytes 11011072 | tf_op jit(solution)/shard_map/while/body/eval_jaxpr/kpc,cw->kpw/dot_general | solution.py:115
  30.2 0.6 fusion.115
  30.8 4.3 %fusion.116 = f32[1,128,1024]{2,0,1:T(1,128)S(1)} fusion(f32[4,128,1024]{2,1,0:T(8,128)S(1)} %fusion.115, f32[4,4]{1,0:T(4,128)S(1)} %get-tuple-element.262, s32[]{:T(128)} %get-tuple-element.251), kind=kOutput, calls=%fused_computation.19.clone.1 | convolution fusion | flops 6291456 | bytes 2621956 | tf_op jit(solution)/shard_map/while/body/eval_jaxpr/k,kpw->pw/dot_general | solution.py:117
  35.4 6.1 %bitcast_dynamic-update-slice_fusion.2 = (f32[4,4,128,2048]{3,2,1,0:T(8,128)}, f32[4,128,2048]{2,1,0:T(8,128)S(1)}) fusion(f32[4,4,128,2048]{3,2,1,0:T(8,128)} %get-tuple-element.253, s32[]{:T(128)} %get-tuple-element.251, f32[256,2048]{1,0:T(8,128)S(1)} %get-tuple-element.264, f32[4,4,128,256]{2,3,1,0:T(8,128)} %get-tuple-element.263), kind=kOutput, calls=%fused_computation.13.clone.1 | convolution fusion | flops 3221225472 | bytes 11011072 | tf_op jit(solution)/shard_map/while/body/eval_jaxpr/kpc,cw->kpw/dot_general | solution.py:115
  41.5 0.6 fusion.115
  42.1 4.3 %fusion.116 = f32[1,128,1024]{2,0,1:T(1,128)S(1)} fusion(f32[4,128,1024]{2,1,0:T(8,128)S(1)} %fusion.115, f32[4,4]{1,0:T(4,128)S(1)} %get-tuple-element.262, s32[]{:T(128)} %get-tuple-element.251), kind=kOutput, calls=%fused_computation.19.clone.1 | convolution fusion | flops 6291456 | bytes 2621956 | tf_op jit(solution)/shard_map/while/body/eval_jaxpr/k,kpw->pw/dot_general | solution.py:117
  46.7 6.1 %bitcast_dynamic-update-slice_fusion.2 = (f32[4,4,128,2048]{3,2,1,0:T(8,128)}, f32[4,128,2048]{2,1,0:T(8,128)S(1)}) fusion(f32[4,4,128,2048]{3,2,1,0:T(8,128)} %get-tuple-element.253, s32[]{:T(128)} %get-tuple-element.251, f32[256,2048]{1,0:T(8,128)S(1)} %get-tuple-element.264, f32[4,4,128,256]{2,3,1,0:T(8,128)} %get-tuple-element.263), kind=kOutput, calls=%fused_computation.13.clone.1 | convolution fusion | flops 3221225472 | bytes 11011072 | tf_op jit(solution)/shard_map/while/body/eval_jaxpr/kpc,cw->kpw/dot_general | solution.py:115
  52.8 0.6 fusion.115
  53.4 4.3 %fusion.116 = f32[1,128,1024]{2,0,1:T(1,128)S(1)} fusion(f32[4,128,1024]{2,1,0:T(8,128)S(1)} %fusion.115, f32[4,4]{1,0:T(4,128)S(1)} %get-tuple-element.262, s32[]{:T(128)} %get-tuple-element.251), kind=kOutput, calls=%fused_computation.19.clone.1 | convolution fusion | flops 6291456 | bytes 2621956 | tf_op jit(solution)/shard_map/while/body/eval_jaxpr/k,kpw->pw/dot_general | solution.py:117
  58.0 6.1 %bitcast_dynamic-update-slice_fusion.2 = (f32[4,4,128,2048]{3,2,1,0:T(8,128)}, f32[4,128,2048]{2,1,0:T(8,128)S(1)}) fusion(f32[4,4,128,2048]{3,2,1,0:T(8,128)} %get-tuple-element.253, s32[]{:T(128)} %get-tuple-element.251, f32[256,2048]{1,0:T(8,128)S(1)} %get-tuple-element.264, f32[4,4,128,256]{2,3,1,0:T(8,128)} %get-tuple-element.263), kind=kOutput, calls=%fused_computation.13.clone.1 | convolution fusion | flops 3221225472 | bytes 11011072 | tf_op jit(solution)/shard_map/while/body/eval_jaxpr/kpc,cw->kpw/dot_general | solution.py:115
  64.1 0.6 fusion.115
  64.7 4.3 %fusion.116 = f32[1,128,1024]{2,0,1:T(1,128)S(1)} fusion(f32[4,128,1024]{2,1,0:T(8,128)S(1)} %fusion.115, f32[4,4]{1,0:T(4,128)S(1)} %get-tuple-element.262, s32[]{:T(128)} %get-tuple-element.251), kind=kOutput, calls=%fused_computation.19.clone.1 | convolution fusion | flops 6291456 | bytes 2621956 | tf_op jit(solution)/shard_map/while/body/eval_jaxpr/k,kpw->pw/dot_general | solution.py:117
  69.2 2.1 %subtract_multiply_fusion = (f32[128,1024]{1,0:T(8,128)S(1)}, f32[128,1024]{1,0:T(8,128)}) fusion(s32[128,1024]{1,0:T(8,128)} %param.13, f32[128,1024]{1,0:T(8,128)S(1)} %get-tuple-element.91), kind=kLoop, calls=%fused_computation.62 | loop fusion | flops 1441792 | bytes 2097152 | tf_op jit(solution)/shard_map/mul | solution.py:123
  71.4 26.6 %while.25 = (s32[]{:T(128)}, f32[4,4,128,256]{3,2,1,0:T(8,128)}, f32[4,4]{1,0:T(4,128)S(1)}, f32[128,2048]{1,0:T(8,128)S(1)}, f32[4,4,128,2048]{3,2,1,0:T(8,128)}, /*index=5*/f32[256,2048]{1,0:T(8,128)S(1)}, s32[]{:T(128)}) while((s32[]{:T(128)}, f32[4,4,128,256]{3,2,1,0:T(8,128)}, f32[4,4]{1,0:T(4,128)S(1)}, f32[128,2048]{1,0:T(8,128)S(1)}, ...), condition=%wide.region_4.5_spmd, body=%wide.region_3.4_spmd.sunk | while | flops 3223322624 | bytes 7865473 | solution.py:131
  71.4 6.6 %fusion.112 = f32[4,4,128,256]{3,2,1,0:T(8,128)} fusion(f32[4,4,128,256]{3,2,1,0:T(8,128)} %get-tuple-element.275, s32[]{:T(128)} %get-tuple-element.274, f32[256,2048]{1,0:T(8,128)S(1)} %get-tuple-element.286, f32[4,4,128,2048]{3,2,1,0:T(8,128)} %get-tuple-element.285, f32[128,2048]{1,0:T(8,128)S(1)} %get-tuple-element.284, f32[4]{0:T(128)S(1)} %fusion.111), kind=kOutput, calls=%fused_computation.8.clone.1 | convolution fusion | flops 3223322624 | bytes 7865360 | tf_op jit(solution)/shard_map/while/body/eval_jaxpr/kpw,cw->kpc/dot_general | solution.py:129
  78.1 6.6 %fusion.112 = f32[4,4,128,256]{3,2,1,0:T(8,128)} fusion(f32[4,4,128,256]{3,2,1,0:T(8,128)} %get-tuple-element.275, s32[]{:T(128)} %get-tuple-element.274, f32[256,2048]{1,0:T(8,128)S(1)} %get-tuple-element.286, f32[4,4,128,2048]{3,2,1,0:T(8,128)} %get-tuple-element.285, f32[128,2048]{1,0:T(8,128)S(1)} %get-tuple-element.284, f32[4]{0:T(128)S(1)} %fusion.111), kind=kOutput, calls=%fused_computation.8.clone.1 | convolution fusion | flops 3223322624 | bytes 7865360 | tf_op jit(solution)/shard_map/while/body/eval_jaxpr/kpw,cw->kpc/dot_general | solution.py:129
  84.7 6.7 %fusion.112 = f32[4,4,128,256]{3,2,1,0:T(8,128)} fusion(f32[4,4,128,256]{3,2,1,0:T(8,128)} %get-tuple-element.275, s32[]{:T(128)} %get-tuple-element.274, f32[256,2048]{1,0:T(8,128)S(1)} %get-tuple-element.286, f32[4,4,128,2048]{3,2,1,0:T(8,128)} %get-tuple-element.285, f32[128,2048]{1,0:T(8,128)S(1)} %get-tuple-element.284, f32[4]{0:T(128)S(1)} %fusion.111), kind=kOutput, calls=%fused_computation.8.clone.1 | convolution fusion | flops 3223322624 | bytes 7865360 | tf_op jit(solution)/shard_map/while/body/eval_jaxpr/kpw,cw->kpc/dot_general | solution.py:129
  91.3 6.6 %fusion.112 = f32[4,4,128,256]{3,2,1,0:T(8,128)} fusion(f32[4,4,128,256]{3,2,1,0:T(8,128)} %get-tuple-element.275, s32[]{:T(128)} %get-tuple-element.274, f32[256,2048]{1,0:T(8,128)S(1)} %get-tuple-element.286, f32[4,4,128,2048]{3,2,1,0:T(8,128)} %get-tuple-element.285, f32[128,2048]{1,0:T(8,128)S(1)} %get-tuple-element.284, f32[4]{0:T(128)S(1)} %fusion.111), kind=kOutput, calls=%fused_computation.8.clone.1 | convolution fusion | flops 3223322624 | bytes 7865360 | tf_op jit(solution)/shard_map/while/body/eval_jaxpr/kpw,cw->kpc/dot_general | solution.py:129
  98.0 3.0 %convolution_bitcast_fusion = f32[16,64,256]{2,1,0:T(8,128)S(1)} fusion(f32[16,128,256]{2,1,0:T(8,128)} %bitcast.113, f32[32,256]{1,0:T(8,128)S(1)} %get-tuple-element.161, f32[32,256]{1,0:T(8,128)S(1)} %get-tuple-element.162), kind=kOutput, calls=%fused_computation.28 | convolution fusion | flops 402661376 | bytes 3211264 | tf_op jit(solution)/shard_map/pr,kpc->krc/dot_general | solution.py:79
  101.2 4.4 %collective-permute-start.3 = (f32[1,64,256]{2,1,0:T(8,128)S(1)}, f32[1,64,256]{2,1,0:T(8,128)S(1)}, u32[]{:S(2)}, u32[]{:S(2)}) collective-permute-start(f32[1,64,256]{2,1,0:T(8,128)S(1)} %fusion.68), channel_id=1, source_target_pairs={{1,0},{2,1},{3,2},{4,3},{5,4},{6,5},{7,6},{8,7},{9,8},{10,9},{11,1... | collective-permute-start | bytes 196616 | tf_op jit(solution)/shard_map/ppermute | solution.py:25
  106.1 1.6 %collective-permute-done.2 = f32[1,64,256]{2,1,0:T(8,128)S(1)} collective-permute-done((f32[1,64,256]{2,1,0:T(8,128)S(1)}, f32[1,64,256]{2,1,0:T(8,128)S(1)}, u32[]{:S(2)}, u32[]{:S(2)}) %collective-permute-start.2) | collective-permute-done | bytes 65568 | tf_op jit(solution)/shard_map/ppermute | solution.py:22
  108.3 1.9 %convolution_multiply_fusion = f32[128,1024]{1,0:T(8,128)} fusion(f32[128,256]{1,0:T(8,128)S(1)} %fusion.25, f32[1024,128]{1,0:T(8,128)S(1)} %copy-done.4, f32[1024,128]{1,0:T(8,128)S(1)} %copy-done.2, f32[128,1024]{1,0:T(8,128)S(1)} %copy-done), kind=kOutput, calls=%fused_computation.29 | convolution fusion | flops 403570688 | bytes 2228224 | tf_op jit(solution)/shard_map/dot_general | solution.py:31
  (49 shorter events, 3.9 us)
Async XLA Ops:
  0.6 10.8 %copy-start.8 = (f32[16]{0:T(128)S(1)}, f32[16]{0:T(128)}, u32[]{:S(2)}) copy-start(f32[16]{0:T(128)} %param.15) | copy-start | bytes 196
  1.8 6.3 %copy-start.7 = (f32[128,1024]{1,0:T(8,128)}, f32[128,1024]{1,0:T(8,128)S(1)}, u32[]{:S(2)}) copy-start(f32[128,1024]{1,0:T(8,128)S(1)} %tanh.3) | copy-start | bytes 1572868
  2.6 13.7 %collective-permute-start = (f32[64,1024]{1,0:T(8,128)}, f32[64,1024]{1,0:T(8,128)}, u32[]{:S(2)}, u32[]{:S(2)}) collective-permute-start(f32[64,1024]{1,0:T(8,128)} %get-tuple-element.154), channel_id=1, source_target_pairs={{0,1},{1,2},{2,3},{3,4},{4,5},{5,6},{6,7},{7,8},{8,9},{9,10},{10,1... | collective-permute-start | bytes 786440 | tf_op jit(solution)/shard_map/ppermute | solution.py:22
  3.1 13.3 %collective-permute-start.1 = (f32[64,1024]{1,0:T(8,128)S(1)}, f32[64,1024]{1,0:T(8,128)}, u32[]{:S(2)}, u32[]{:S(2)}) collective-permute-start(f32[64,1024]{1,0:T(8,128)S(1)} %get-tuple-element.155), channel_id=1, source_target_pairs={{1,0},{2,1},{3,2},{4,3},{5,4},{6,5},{7,6},{8,7},{9,8},{10,9},{11,1... | collective-permute-start | bytes 786440 | tf_op jit(solution)/shard_map/ppermute | solution.py:25
  14.2 5.0 %copy-start.5 = (f32[2,16,32,128]{3,2,1,0:T(8,128)S(1)}, f32[2,16,32,128]{3,2,1,0:T(8,128)}, u32[]{:S(2)}) copy-start(f32[2,16,32,128]{3,2,1,0:T(8,128)} %param.14) | copy-start | bytes 1572868
  16.3 3.0 %copy-start.1 = (f32[1024,128]{1,0:T(8,128)}, f32[1024,128]{1,0:T(8,128)S(1)}, u32[]{:S(2)}) copy-start(f32[1024,128]{1,0:T(8,128)S(1)} %get-tuple-element.163) | copy-start | bytes 1572868
  16.3 3.0 %copy-start.3 = (f32[1024,128]{1,0:T(8,128)}, f32[1024,128]{1,0:T(8,128)S(1)}, u32[]{:S(2)}) copy-start(f32[1024,128]{1,0:T(8,128)S(1)} %get-tuple-element.164) | copy-start | bytes 1572868
  98.0 3.1 %copy-start.6 = (f32[2,16,32,128]{3,2,1,0:T(8,128)S(1)}, f32[2,16,32,128]{3,2,1,0:T(8,128)}, u32[]{:S(2)}) copy-start(f32[2,16,32,128]{3,2,1,0:T(8,128)} %param.14) | copy-start | bytes 1572868
  98.0 10.3 %copy-start = (f32[128,1024]{1,0:T(8,128)S(1)}, f32[128,1024]{1,0:T(8,128)}, u32[]{:S(2)}) copy-start(f32[128,1024]{1,0:T(8,128)} %param.12) | copy-start | bytes 1572868
  98.0 10.3 %copy-start.2 = (f32[1024,128]{1,0:T(8,128)S(1)}, f32[1024,128]{1,0:T(8,128)}, u32[]{:S(2)}) copy-start(f32[1024,128]{1,0:T(8,128)} %copy-done.1) | copy-start | bytes 1572868
  98.0 10.3 %copy-start.4 = (f32[1024,128]{1,0:T(8,128)S(1)}, f32[1024,128]{1,0:T(8,128)}, u32[]{:S(2)}) copy-start(f32[1024,128]{1,0:T(8,128)} %copy-done.3) | copy-start | bytes 1572868
  101.2 6.4 %collective-permute-start.2 = (f32[1,64,256]{2,1,0:T(8,128)S(1)}, f32[1,64,256]{2,1,0:T(8,128)S(1)}, u32[]{:S(2)}, u32[]{:S(2)}) collective-permute-start(f32[1,64,256]{2,1,0:T(8,128)S(1)} %fusion.68), channel_id=1, source_target_pairs={{0,1},{1,2},{2,3},{3,4},{4,5},{5,6},{6,7},{7,8},{8,9},{9,10},{10,1... | collective-permute-start | bytes 196616 | tf_op jit(solution)/shard_map/ppermute | solution.py:22
  101.2 6.7 %collective-permute-start.3 = (f32[1,64,256]{2,1,0:T(8,128)S(1)}, f32[1,64,256]{2,1,0:T(8,128)S(1)}, u32[]{:S(2)}, u32[]{:S(2)}) collective-permute-start(f32[1,64,256]{2,1,0:T(8,128)S(1)} %fusion.68), channel_id=1, source_target_pairs={{1,0},{2,1},{3,2},{4,3},{5,4},{6,5},{7,6},{8,7},{9,8},{10,9},{11,1... | collective-permute-start | bytes 196616 | tf_op jit(solution)/shard_map/ppermute | solution.py:25
where the time goes:
time: 111 us; the launch traced here: 110 us
  matrix products  81.7 us (74%)
  other arithmetic  13.8 us (12%)
  starting transfers between devices  9.93 us (9%)
  local copies, waits for them, and re-layouts  2.06 us (2%)
  waiting for transfers between devices  1.56 us (1%)
    dot_general x4, matrix products, adjoint_block(): jnp.einsum('kpw,cw->kpc', field_grad, inverse_cols, precision=HIGHEST)  26.5 us
    dot_general x4, matrix products, add_power(): jnp.einsum('kpc,cw->kpw', inner_block, inverse_cols, precision=HIGHEST)  24.5 us
    dot_general x4, matrix products, add_power(): jnp.einsum('k,kpw->pw', share_block, powers, precision=HIGHEST)  17.2 us
    ppermute x2, starting transfers between devices, with_halo(): lax.ppermute(lax.slice_in_dim(block, 0, width, axis=dim), axis, backward)  9.42 us
    dot_general x6, matrix products, matmul(): jnp.dot(left, right, precision=HIGHEST, preferred_element_type=jnp.float32)  5.73 us
    dot_general x1, matrix products, kernel_fields(): return jnp.einsum('pr,krc->kpc', own_rows, blocked, precision=HIGHEST)  4.79 us
    sin x1, other arithmetic, phase_table(): return (jnp.cos(angles), jnp.sin(angles))  3.15 us
    dot_general x1, matrix products, window_adjoint(): jnp.einsum('pr,kpc->krc', own_rows, inner_grad, precision=HIGHEST)  3.04 us
  transfers between devices with their start and end apart: 4, of which 1 were waited for; matrix products, arithmetic and copies ran while one was open for 8% of the time, Pallas kernels for 0%

commit v1 on v0

v1 whole, which is shorter than its diff:
```python
import functools
import math

import jax
import jax.numpy as jnp
import ml_dtypes
import numpy as np
from jax import lax
from jax.experimental import pallas as pl
from jax.experimental.pallas import tpu as pltpu
from jax.sharding import PartitionSpec as P

MARGIN = 64
STEEPNESS = 8.0
THRESHOLD = 0.35
GROUP = 4
MESH = pl.DeviceIdType.MESH


def split_table(table):
    high = table.astype(ml_dtypes.bfloat16)
    low = (table - high.astype(np.float64)).astype(ml_dtypes.bfloat16)
    return high, low


def deep_table(table):
    high, low = split_table(table)
    return np.concatenate([high, high, low], axis=1)


def cos_sin(frequencies, positions):
    angles = 2.0 * math.pi * np.outer(frequencies, positions)
    return np.cos(angles), np.sin(angles)


def interpolation(half_band, coarse, fine_positions):
    degrees = np.arange(1, half_band)
    offsets = fine_positions[:, None] - (np.arange(coarse) / coarse)[None, :]
    waves = np.cos(2.0 * math.pi * offsets[:, :, None] * degrees).sum(axis=2)
    return (1.0 + 2.0 * waves) / coarse


def make_tables(strip_rows, columns, freq_rows, freq_cols):
    margin = MARGIN
    window = strip_rows + 2 * margin
    col_freq = np.arange(freq_cols) - freq_cols // 2
    row_freq = np.arange(freq_rows) - freq_rows // 2
    col_cos, col_sin = cos_sin(col_freq, np.arange(columns) / columns)
    row_cos, row_sin = cos_sin(row_freq, np.arange(window) / window)
    factor = 1.0 / math.sqrt(window * columns)
    forward = np.concatenate([col_cos.T, -col_sin.T], axis=1) * factor
    stack = np.concatenate([row_cos, row_sin], axis=0)
    own = stack[:, margin : margin + strip_rows]
    to_prev = np.zeros_like(own)
    to_prev[:, :margin] = stack[:, margin + strip_rows :]
    to_next = np.zeros_like(own)
    to_next[:, strip_rows - margin :] = stack[:, :margin]
    rows_in = np.concatenate([to_prev, to_next, own], axis=0)
    rows_near = np.concatenate([to_prev, to_next], axis=0).T
    coarse_rows, coarse_cols = 2 * freq_rows, 2 * freq_cols
    ccos, csin = cos_sin(col_freq, np.arange(coarse_cols) / coarse_cols)
    rcos, rsin = cos_sin(row_freq, np.arange(coarse_rows) / coarse_rows)
    inverse = np.concatenate([ccos, -csin], axis=0)
    rows_out = np.concatenate(
        [np.concatenate([rcos.T, -rsin.T], axis=1), np.concatenate([rsin.T, rcos.T], axis=1)],
        axis=0,
    )
    own_positions = (margin + np.arange(strip_rows)) / window
    up_rows = interpolation(freq_rows, coarse_rows, own_positions)
    up_cols = interpolation(freq_cols, coarse_cols, np.arange(columns) / columns).T
    return {
        "forward": np.stack(split_table(forward)),
        "rows_in": deep_table(rows_in),
        "inverse": np.stack(split_table(inverse)),
        "rows_out": deep_table(rows_out),
        "up_cols": np.stack(split_table(up_cols)),
        "up_rows": deep_table(up_rows),
        "down_rows": deep_table(up_rows.T),
        "down_cols": np.stack(split_table(up_cols.T)),
        "rows_back": deep_table(rows_out.T),
        "inverse_back": np.stack(split_table(inverse.T)),
        "rows_own": deep_table(own.T),
        "rows_near": deep_table(rows_near),
        "forward_back": np.stack(split_table(forward.T)),
    }


def split(values):
    high = values.astype(jnp.bfloat16)
    low = (values - high.astype(jnp.float32)).astype(jnp.bfloat16)
    return high, low


def dot(left, right):
    return jnp.dot(left, right, preferred_element_type=jnp.float32)


def times_table(values, table):
    rows = values.shape[0]
    high, low = split(values)
    both = dot(jnp.concatenate([high, low], axis=0), table[0])
    return both[:rows] + (both[rows:] + dot(high, table[1]))


def table_times(deep, values):
    high, low = split(values)
    return dot(deep, jnp.concatenate([high, low, high], axis=0))


def fold(product):
    half_rows, half_cols = product.shape[0] // 2, product.shape[1] // 2
    real = product[:half_rows, :half_cols] + product[half_rows:, half_cols:]
    imag = product[:half_rows, half_cols:] - product[half_rows:, :half_cols]
    return jnp.concatenate([real, imag], axis=1)


def unfold(spectrum):
    half = spectrum.shape[1] // 2
    real, imag = spectrum[:, :half], spectrum[:, half:]
    return jnp.concatenate(
        [spectrum, jnp.concatenate([-imag, real], axis=1)], axis=0
    )


def kernel(count, names, weights_ref, mask_hbm, target_hbm, spectra_hbm, *refs):
    tables_hbm = refs[: len(names)]
    refs = refs[len(names) :]
    resist_hbm, grad_hbm = refs[:2]
    refs = refs[2:]
    tables = dict(zip(names, refs[: len(names)]))
    refs = refs[len(names) :]
    (mask, target, spectra, transmit, fields, resist, grad,
     send1, recv1, send2, recv2, in_sem, out_sem, send_sem, recv_sem) = refs

    me = lax.axis_index("tiles")
    following = lax.rem(me + 1, count)
    previous = lax.rem(me + count - 1, count)
    barrier = pltpu.get_barrier_semaphore()
    for other in (previous, following):
        pl.semaphore_signal(barrier, inc=1, device_id={"tiles": other}, device_id_type=MESH)

    sources = {"mask": (mask_hbm, mask), "spectra": (spectra_hbm, spectra), "target": (target_hbm, target)}
    for name, source in zip(names, tables_hbm):
        sources[name] = (source, tables[name])
    order = ["mask", "forward", "rows_in", "spectra", "inverse", "rows_out", "up_cols",
             "up_rows", "target", "down_rows", "down_cols", "rows_back", "inverse_back",
             "rows_own", "rows_near", "forward_back"]
    loads = {}
    for at, name in enumerate(order):
        loads[name] = pltpu.make_async_copy(*sources[name], in_sem.at[at])
        loads[name].start()

    def table(name):
        loads[name].wait()
        return tables[name]

    def swap(step, to_previous, to_following):
        landed = recv1 if step == 0 else recv2
        copies = [
            pltpu.make_async_remote_copy(
                src_ref=to_following, dst_ref=landed.at[0],
                send_sem=send_sem.at[2 * step], recv_sem=recv_sem.at[2 * step],
                device_id={"tiles": following}, device_id_type=MESH),
            pltpu.make_async_remote_copy(
                src_ref=to_previous, dst_ref=landed.at[1],
                send_sem=send_sem.at[2 * step + 1], recv_sem=recv_sem.at[2 * step + 1],
                device_id={"tiles": previous}, device_id_type=MESH),
        ]
        for copy in copies:
            copy.start()
        return copies

    loads["mask"].wait()
    transmit[...] = jnp.tanh(mask[...])
    column_spec = times_table(transmit[...], table("forward"))
    product = table_times(table("rows_in")[...], column_spec)
    span = product.shape[0] // 3
    send1[0] = fold(product[:span])
    send1[1] = fold(product[span : 2 * span])
    pl.semaphore_wait(barrier, 2)
    copies = swap(0, send1.at[0], send1.at[1])
    own_spec = fold(product[2 * span :])

    kernels, freq_rows, freq_cols = spectra.shape[1:]
    loads["spectra"].wait()
    weights = [jnp.full((1, freq_cols), weights_ref[k], jnp.float32) for k in range(kernels)]
    total = functools.reduce(jnp.add, weights)
    for k in range(kernels):
        scale = jnp.sqrt(weights[k] / total)
        spectra[0, k] = spectra[0, k] * scale
        spectra[1, k] = spectra[1, k] * scale
    inverse, rows_out = table("inverse"), table("rows_out")

    for copy in copies:
        copy.wait()
    spec = own_spec + (recv1[0] + recv1[1])
    spec_real, spec_imag = spec[:, :freq_cols], spec[:, freq_cols:]

    depth = 2 * freq_rows
    coarse = fields.shape[1] // 2
    power = None
    for first in range(0, kernels, GROUP):
        members = range(first, min(first + GROUP, kernels))
        blocks = []
        for k in members:
            real = spectra[0, k] * spec_real - spectra[1, k] * spec_imag
            imag = spectra[0, k] * spec_imag + spectra[1, k] * spec_real
            blocks.append(jnp.concatenate([real, imag], axis=1))
            blocks.append(jnp.concatenate([imag, -real], axis=1))
        across = times_table(jnp.concatenate(blocks, axis=0), inverse)
        for place, k in enumerate(members):
            field = table_times(rows_out[...], across[place * depth : (place + 1) * depth])
            fields[k] = field
            term = field[:coarse] * field[:coarse] + field[coarse:] * field[coarse:]
            power = term if power is None else power + term

    intensity = table_times(table("up_rows")[...], times_table(power, table("up_cols")))
    image = jax.nn.sigmoid(STEEPNESS * (intensity - THRESHOLD))
    resist[...] = image
    store_resist = pltpu.make_async_copy(resist, resist_hbm, out_sem.at[0])
    store_resist.start()
    loads["target"].wait()
    slopes = (4.0 * STEEPNESS) * (image - target[...].astype(jnp.float32)) * image * (1.0 - image)
    slopes = times_table(table_times(table("down_rows")[...], slopes), table("down_cols"))
    slopes = jnp.concatenate([slopes, slopes], axis=0)

    rows_back, inverse_back = table("rows_back"), table("inverse_back")
    grad_real = grad_imag = None
    for first in range(0, kernels, GROUP):
        members = range(first, min(first + GROUP, kernels))
        blocks = [table_times(rows_back[...], fields[k] * slopes) for k in members]
        across = times_table(jnp.concatenate(blocks, axis=0), inverse_back)
        for place, k in enumerate(members):
            upper = across[place * depth : place * depth + freq_rows]
            lower = across[place * depth + freq_rows : (place + 1) * depth]
            real = upper[:, :freq_cols] - lower[:, freq_cols:]
            imag = upper[:, freq_cols:] + lower[:, :freq_cols]
            term_real = real * spectra[0, k] + imag * spectra[1, k]
            term_imag = imag * spectra[0, k] - real * spectra[1, k]
            grad_real = term_real if grad_real is None else grad_real + term_real
            grad_imag = term_imag if grad_imag is None else grad_imag + term_imag
    window_grad = jnp.concatenate([grad_real, grad_imag], axis=1)
    send2[...] = window_grad
    copies = swap(1, send2, send2)
    merged = table_times(table("rows_own")[...], unfold(window_grad))
    rows_near, forward_back = table("rows_near"), table("forward_back")
    for copy in copies:
        copy.wait()
    near = jnp.concatenate([unfold(recv2[0]), unfold(recv2[1])], axis=0)
    merged = merged + table_times(rows_near[...], near)
    held = transmit[...]
    grad[...] = times_table(merged, forward_back) * (1.0 - held * held)
    store_grad = pltpu.make_async_copy(grad, grad_hbm, out_sem.at[1])
    store_grad.start()
    store_resist.wait()
    store_grad.wait()


def shards(count, mask_params, target, kernel_spectra, kernel_weights):
    strip_rows, columns = mask_params.shape
    kernels, freq_rows, freq_cols = kernel_spectra.shape[1:]
    tables = make_tables(strip_rows, columns, freq_rows, freq_cols)
    names = list(tables)
    spectrum = (freq_rows, 2 * freq_cols)
    anywhere = pl.BlockSpec(memory_space=pl.ANY)
    out = jax.ShapeDtypeStruct((strip_rows, columns), jnp.float32)
    return pl.pallas_call(
        functools.partial(kernel, count, names),
        out_shape=(out, out),
        in_specs=[pl.BlockSpec(memory_space=pltpu.SMEM)] + [anywhere] * (3 + len(names)),
        out_specs=(anywhere, anywhere),
        scratch_shapes=[pltpu.VMEM(t.shape, jnp.bfloat16) for t in tables.values()]
        + [
            pltpu.VMEM((strip_rows, columns), jnp.float32),
            pltpu.VMEM((strip_rows, columns), jnp.int32),
            pltpu.VMEM(kernel_spectra.shape, jnp.float32),
            pltpu.VMEM((strip_rows, columns), jnp.float32),
            pltpu.VMEM((kernels, 4 * freq_rows, 2 * freq_cols), jnp.float32),
            pltpu.VMEM((strip_rows, columns), jnp.float32),
            pltpu.VMEM((strip_rows, columns), jnp.float32),
            pltpu.VMEM((2,) + spectrum, jnp.float32),
            pltpu.VMEM((2,) + spectrum, jnp.float32),
            pltpu.VMEM(spectrum, jnp.float32),
            pltpu.VMEM((2,) + spectrum, jnp.float32),
            pltpu.SemaphoreType.DMA((3 + len(names),)),
            pltpu.SemaphoreType.DMA((2,)),
            pltpu.SemaphoreType.DMA((4,)),
            pltpu.SemaphoreType.DMA((4,)),
        ],
        compiler_params=pltpu.CompilerParams(
            collective_id=0, has_side_effects=True, vmem_limit_bytes=56 * 1024 * 1024
        ),
        name="litho_step",
    )(kernel_weights, mask_params, target, kernel_spectra, *[jnp.asarray(t) for t in tables.values()])


def solution(mesh):
    rows = P(("parts", "tiles"), None)
    body = functools.partial(shards, mesh.shape["tiles"])
    return jax.shard_map(
        body, mesh=mesh, in_specs=(rows, rows, P(), P()), out_specs=(rows, rows), check_vma=False
    )
```

time: 111 us -> 23.4 us (0.21)
  matrix products: 81.7 us -> 0 us
  Pallas kernels: 0 us -> 19.9 us
  other arithmetic: 13.8 us -> 0 us
  starting transfers between devices: 9.93 us -> 0 us
  waiting for transfers between devices: 1.56 us -> 0 us
    dot_general x20 -> x0, matrix products: 81.7 us -> none  [the longest x4 26.5 us: adjoint_block(): jnp.einsum('kpw,cw->kpc', field_grad, inverse_cols, precision=HIGHEST)]
    pallas_call x0 -> x1, Pallas kernels: none -> 19.9 us  [shards(): pl.pallas_call(functools.partial(kernel, count, names), out_shape=(out, o...]
    ppermute x4 -> x0, starting transfers between devices: 9.93 us -> none  [the longest x2 9.42 us: with_halo(): lax.ppermute(lax.slice_in_dim(block, 0, width, axis=dim), axis, backward)]
    add x9 -> x0, other arithmetic: 3.31 us -> none  [the longest x4 2.52 us: add_power(): powers = fields[:, :, :columns] ** 2 + fields[:, :, columns:] ** 2]
    sin x1 -> x0, other arithmetic: 3.15 us -> none  [phase_table(): return (jnp.cos(angles), jnp.sin(angles))]
    unnamed x18 -> x4, local copies, waits for them, and re-layouts: 0.04 us -> 2.74 us
    cos x2 -> x0, other arithmetic: 2.29 us -> none  [phase_table(): return (jnp.cos(angles), jnp.sin(angles))]
    mul x5 -> x0, other arithmetic: 2.08 us -> none  [the longest x1 2.06 us: shards(): 2.0 * (resist - target.astype(jnp.float32)) * STEEPNESS * resist]
  transfers between devices with their start and end apart: 4 -> 0, of which waited for: 1 -> 0; matrix products, arithmetic and copies ran while one was open for 8% -> 0% of each run, Pallas kernels for 0% -> 0%
where the time goes in v1:
time: 23.4 us; the launch traced here: 23.3 us
  Pallas kernels  19.9 us (85%)
  local copies, waits for them, and re-layouts  2.74 us (12%)
  between operations  0.65 us (3%)
    pallas_call x1, Pallas kernels, shards(): pl.pallas_call(functools.partial(kernel, count, names), out_shape=(out, o...  19.9 us
    unnamed x4, local copies, waits for them, and re-layouts  2.74 us

profile of v1, /device:TPU:0, one launch (start us, length us, event | category | flops | bytes accessed | tf_op | source)
XLA Modules:
  0.0 23.3 jit_solution(12614778603535654330)
XLA Ops:
  0.6 19.9 %litho_step.1 = (f32[128,1024]{1,0:T(8,128)}, f32[128,1024]{1,0:T(8,128)}) custom-call(f32[16]{0:T(128)} %weights_ref.1, f32[128,1024]{1,0:T(8,128)} %mask_hbm.1, s32[128,1024]{1,0:T(8,128)} %target_hbm.1, f32[2,16,32,128]{3,2,1,0:T(8,128)} %spectra_hbm.1, bf16[2,1024,256]{2,1,0:T(8,128)(2,1)} %constant.26.clone.refs_0_, ...), custom_call_target="tpu_custom_call" | custom-call | tf_op jit(solution)/shard_map/litho_step/pallas_call | solution.py:267
  20.5 0.0 copy-start
  20.5 1.9 %copy.21 = f32[128,1024]{1,0:T(8,128)} copy(f32[128,1024]{1,0:T(8,128)} %get-tuple-element.4) | data formatting | bytes 1048576
  22.5 0.0 copy-done
  22.5 0.8 %copy.22 = f32[128,1024]{1,0:T(8,128)} copy(f32[128,1024]{1,0:T(8,128)S(1)} %copy-done) | data formatting | bytes 1048576
Async XLA Ops:
  20.5 2.0 %copy-start = (f32[128,1024]{1,0:T(8,128)S(1)}, f32[128,1024]{1,0:T(8,128)}, u32[]{:S(2)}) copy-start(f32[128,1024]{1,0:T(8,128)} %get-tuple-element.5) | copy-start | bytes 1572868

commit v2 on v1

--- a/solution.py
+++ b/solution.py
@@ -60,7 +60,9 @@
     coarse_rows, coarse_cols = 2 * freq_rows, 2 * freq_cols
     ccos, csin = cos_sin(col_freq, np.arange(coarse_cols) / coarse_cols)
     rcos, rsin = cos_sin(row_freq, np.arange(coarse_rows) / coarse_rows)
-    inverse = np.concatenate([ccos, -csin], axis=0)
+    inverse = np.concatenate(
+        [np.concatenate([ccos, csin], axis=1), np.concatenate([-csin, ccos], axis=1)], axis=0
+    )
     rows_out = np.concatenate(
         [np.concatenate([rcos.T, -rsin.T], axis=1), np.concatenate([rsin.T, rcos.T], axis=1)],
         axis=0,
@@ -148,6 +150,7 @@
     loads = {}
     for at, name in enumerate(order):
         loads[name] = pltpu.make_async_copy(*sources[name], in_sem.at[at])
+    for name in order[:4]:
         loads[name].start()
 
     def table(name):
@@ -172,7 +175,10 @@
 
     loads["mask"].wait()
     transmit[...] = jnp.tanh(mask[...])
-    column_spec = times_table(transmit[...], table("forward"))
+    forward = table("forward")
+    for name in order[4:]:
+        loads[name].start()
+    column_spec = times_table(transmit[...], forward)
     product = table_times(table("rows_in")[...], column_spec)
     span = product.shape[0] // 3
     send1[0] = fold(product[:span])
@@ -196,7 +202,6 @@
     spec = own_spec + (recv1[0] + recv1[1])
     spec_real, spec_imag = spec[:, :freq_cols], spec[:, freq_cols:]
 
-    depth = 2 * freq_rows
     coarse = fields.shape[1] // 2
     power = None
     for first in range(0, kernels, GROUP):
@@ -206,10 +211,12 @@
             real = spectra[0, k] * spec_real - spectra[1, k] * spec_imag
             imag = spectra[0, k] * spec_imag + spectra[1, k] * spec_real
             blocks.append(jnp.concatenate([real, imag], axis=1))
-            blocks.append(jnp.concatenate([imag, -real], axis=1))
         across = times_table(jnp.concatenate(blocks, axis=0), inverse)
+        half = across.shape[1] // 2
         for place, k in enumerate(members):
-            field = table_times(rows_out[...], across[place * depth : (place + 1) * depth])
+            part = across[place * freq_rows : (place + 1) * freq_rows]
+            part = jnp.concatenate([part[:, :half], part[:, half:]], axis=0)
+            field = table_times(rows_out[...], part)
             fields[k] = field
             term = field[:coarse] * field[:coarse] + field[coarse:] * field[coarse:]
             power = term if power is None else power + term
@@ -228,13 +235,14 @@
     grad_real = grad_imag = None
     for first in range(0, kernels, GROUP):
         members = range(first, min(first + GROUP, kernels))
-        blocks = [table_times(rows_back[...], fields[k] * slopes) for k in members]
+        blocks = []
+        for k in members:
+            part = table_times(rows_back[...], fields[k] * slopes)
+            blocks.append(jnp.concatenate([part[:freq_rows], part[freq_rows:]], axis=1))
         across = times_table(jnp.concatenate(blocks, axis=0), inverse_back)
         for place, k in enumerate(members):
-            upper = across[place * depth : place * depth + freq_rows]
-            lower = across[place * depth + freq_rows : (place + 1) * depth]
-            real = upper[:, :freq_cols] - lower[:, freq_cols:]
-            imag = upper[:, freq_cols:] + lower[:, :freq_cols]
+            part = across[place * freq_rows : (place + 1) * freq_rows]
+            real, imag = part[:, :freq_cols], part[:, freq_cols:]
             term_real = real * spectra[0, k] + imag * spectra[1, k]
             term_imag = imag * spectra[0, k] - real * spectra[1, k]
             grad_real = term_real if grad_real is None else grad_real + term_real

time: 23.4 us -> 23.2 us (level)
  Pallas kernels: 19.9 us -> 19.6 us
    pallas_call x1, Pallas kernels: 19.9 us -> 19.6 us  [shards(): pl.pallas_call(functools.partial(kernel, count, names), out_shape=(out, o...]
where the time goes in v2:
time: 23.2 us; the launch traced here: 23 us
  Pallas kernels  19.6 us (84%)
  local copies, waits for them, and re-layouts  2.74 us (12%)
  between operations  0.65 us (3%)
    pallas_call x1, Pallas kernels, shards(): pl.pallas_call(functools.partial(kernel, count, names), out_shape=(out, o...  19.6 us
    unnamed x4, local copies, waits for them, and re-layouts  2.74 us

profile of v2, /device:TPU:0, one launch (start us, length us, event | category | flops | bytes accessed | tf_op | source)
XLA Modules:
  0.0 23.0 jit_solution(13960389144202367047)
XLA Ops:
  0.6 19.6 %litho_step.1 = (f32[128,1024]{1,0:T(8,128)}, f32[128,1024]{1,0:T(8,128)}) custom-call(f32[16]{0:T(128)} %weights_ref.1, f32[128,1024]{1,0:T(8,128)} %mask_hbm.1, s32[128,1024]{1,0:T(8,128)} %target_hbm.1, f32[2,16,32,128]{3,2,1,0:T(8,128)} %spectra_hbm.1, bf16[2,1024,256]{2,1,0:T(8,128)(2,1)} %constant.26.clone.refs_0_, ...), custom_call_target="tpu_custom_call" | custom-call | tf_op jit(solution)/shard_map/litho_step/pallas_call | solution.py:275
  20.3 0.0 copy-start
  20.3 1.9 %copy.21 = f32[128,1024]{1,0:T(8,128)} copy(f32[128,1024]{1,0:T(8,128)} %get-tuple-element.4) | data formatting | bytes 1048576
  22.2 0.0 copy-done
  22.2 0.8 %copy.22 = f32[128,1024]{1,0:T(8,128)} copy(f32[128,1024]{1,0:T(8,128)S(1)} %copy-done) | data formatting | bytes 1048576
Async XLA Ops:
  20.3 2.0 %copy-start = (f32[128,1024]{1,0:T(8,128)S(1)}, f32[128,1024]{1,0:T(8,128)}, u32[]{:S(2)}) copy-start(f32[128,1024]{1,0:T(8,128)} %get-tuple-element.5) | copy-start | bytes 1572868

commit v3 on v2

--- a/solution.py
+++ b/solution.py
@@ -127,12 +127,12 @@
 def kernel(count, names, weights_ref, mask_hbm, target_hbm, spectra_hbm, *refs):
     tables_hbm = refs[: len(names)]
     refs = refs[len(names) :]
-    resist_hbm, grad_hbm = refs[:2]
+    resist, grad = refs[:2]
     refs = refs[2:]
     tables = dict(zip(names, refs[: len(names)]))
     refs = refs[len(names) :]
-    (mask, target, spectra, transmit, fields, resist, grad,
-     send1, recv1, send2, recv2, in_sem, out_sem, send_sem, recv_sem) = refs
+    (mask, target, spectra, transmit, fields,
+     send1, recv1, send2, recv2, in_sem, send_sem, recv_sem) = refs
 
     me = lax.axis_index("tiles")
     following = lax.rem(me + 1, count)
@@ -224,8 +224,6 @@
     intensity = table_times(table("up_rows")[...], times_table(power, table("up_cols")))
     image = jax.nn.sigmoid(STEEPNESS * (intensity - THRESHOLD))
     resist[...] = image
-    store_resist = pltpu.make_async_copy(resist, resist_hbm, out_sem.at[0])
-    store_resist.start()
     loads["target"].wait()
     slopes = (4.0 * STEEPNESS) * (image - target[...].astype(jnp.float32)) * image * (1.0 - image)
     slopes = times_table(table_times(table("down_rows")[...], slopes), table("down_cols"))
@@ -258,10 +256,17 @@
     merged = merged + table_times(rows_near[...], near)
     held = transmit[...]
     grad[...] = times_table(merged, forward_back) * (1.0 - held * held)
-    store_grad = pltpu.make_async_copy(grad, grad_hbm, out_sem.at[1])
-    store_grad.start()
-    store_resist.wait()
-    store_grad.wait()
+
+
+def store(resist, grad, resist_hbm, grad_hbm, sems):
+    copies = [
+        pltpu.make_async_copy(resist, resist_hbm, sems.at[0]),
+        pltpu.make_async_copy(grad, grad_hbm, sems.at[1]),
+    ]
+    for copy in copies:
+        copy.start()
+    for copy in copies:
+        copy.wait()
 
 
 def shards(count, mask_params, target, kernel_spectra, kernel_weights):
@@ -272,11 +277,13 @@
     spectrum = (freq_rows, 2 * freq_cols)
     anywhere = pl.BlockSpec(memory_space=pl.ANY)
     out = jax.ShapeDtypeStruct((strip_rows, columns), jnp.float32)
-    return pl.pallas_call(
+    held = pltpu.VMEM((strip_rows, columns), jnp.float32)
+    in_vmem = pl.BlockSpec(memory_space=pltpu.VMEM)
+    resist, grad = pl.pallas_call(
         functools.partial(kernel, count, names),
-        out_shape=(out, out),
+        out_shape=(held, held),
         in_specs=[pl.BlockSpec(memory_space=pltpu.SMEM)] + [anywhere] * (3 + len(names)),
-        out_specs=(anywhere, anywhere),
+        out_specs=(in_vmem, in_vmem),
         scratch_shapes=[pltpu.VMEM(t.shape, jnp.bfloat16) for t in tables.values()]
         + [
             pltpu.VMEM((strip_rows, columns), jnp.float32),
@@ -284,14 +291,11 @@
             pltpu.VMEM(kernel_spectra.shape, jnp.float32),
             pltpu.VMEM((strip_rows, columns), jnp.float32),
             pltpu.VMEM((kernels, 4 * freq_rows, 2 * freq_cols), jnp.float32),
-            pltpu.VMEM((strip_rows, columns), jnp.float32),
-            pltpu.VMEM((strip_rows, columns), jnp.float32),
             pltpu.VMEM((2,) + spectrum, jnp.float32),
             pltpu.VMEM((2,) + spectrum, jnp.float32),
             pltpu.VMEM(spectrum, jnp.float32),
             pltpu.VMEM((2,) + spectrum, jnp.float32),
             pltpu.SemaphoreType.DMA((3 + len(names),)),
-            pltpu.SemaphoreType.DMA((2,)),
             pltpu.SemaphoreType.DMA((4,)),
             pltpu.SemaphoreType.DMA((4,)),
         ],
@@ -300,6 +304,14 @@
         ),
         name="litho_step",
     )(kernel_weights, mask_params, target, kernel_spectra, *[jnp.asarray(t) for t in tables.values()])
+    return pl.pallas_call(
+        store,
+        out_shape=(out, out),
+        in_specs=[anywhere, anywhere],
+        out_specs=(anywhere, anywhere),
+        scratch_shapes=[pltpu.SemaphoreType.DMA((2,))],
+        name="store_results",
+    )(resist, grad)
 
 
 def solution(mesh):

time: 23.2 us -> 54.1 us (2.33)
  Pallas kernels: 19.6 us -> 51.7 us
  local copies, waits for them, and re-layouts: 2.74 us -> 1.58 us
    pallas_call x1 -> x2, Pallas kernels: 19.6 us -> 51.7 us  [the longest x1 32.9 us: shards(): pl.pallas_call(store, out_shape=(out, out), in_specs=[anywhere, anywhere]...]
    unnamed x4, local copies, waits for them, and re-layouts: 2.74 us -> 1.58 us
where the time goes in v3:
time: 54.1 us; the launch traced here: 53.9 us
  Pallas kernels  51.7 us (96%)
  local copies, waits for them, and re-layouts  1.58 us (3%)
  between operations  0.65 us (1%)
    pallas_call x1, Pallas kernels, shards(): pl.pallas_call(store, out_shape=(out, out), in_specs=[anywhere, anywhere]...  32.9 us
    pallas_call x1, Pallas kernels, shards(): pl.pallas_call(functools.partial(kernel, count, names), out_shape=(held,...  18.8 us
    unnamed x4, local copies, waits for them, and re-layouts  1.58 us

profile of v3, /device:TPU:0, one launch (start us, length us, event | category | flops | bytes accessed | tf_op | source)
XLA Modules:
  0.0 53.9 jit_solution(7085393419712523381)
XLA Ops:
  0.6 18.8 %litho_step.1 = (f32[128,1024]{1,0:T(8,128)S(1)}, f32[128,1024]{1,0:T(8,128)S(1)}) custom-call(f32[16]{0:T(128)} %weights_ref.1, f32[128,1024]{1,0:T(8,128)} %mask_hbm.1, s32[128,1024]{1,0:T(8,128)} %target_hbm.1, f32[2,16,32,128]{3,2,1,0:T(8,128)} %spectra_hbm.1, bf16[2,1024,256]{2,1,0:T(8,128)(2,1)} %constant.26.clone.refs_0_, ...), custom_call_target="tpu_custom_call" | custom-call | tf_op jit(solution)/shard_map/litho_step/pallas_call | solution.py:282
  19.4 0.0 copy-start
  19.5 0.8 %copy-done = f32[128,1024]{1,0:T(8,128)} copy-done((f32[128,1024]{1,0:T(8,128)}, f32[128,1024]{1,0:T(8,128)S(1)}, u32[]{:S(2)}) %copy-start) | copy-done | bytes 524312
  20.2 0.0 copy-start.1
  20.2 0.8 %copy-done.1 = f32[128,1024]{1,0:T(8,128)} copy-done((f32[128,1024]{1,0:T(8,128)}, f32[128,1024]{1,0:T(8,128)S(1)}, u32[]{:S(2)}) %copy-start.1) | copy-done | bytes 524312
  21.0 32.9 %store_results.1 = (f32[128,1024]{1,0:T(8,128)}, f32[128,1024]{1,0:T(8,128)}) custom-call(f32[128,1024]{1,0:T(8,128)} %copy-done, f32[128,1024]{1,0:T(8,128)} %copy-done.1), custom_call_target="tpu_custom_call" | custom-call | tf_op jit(solution)/shard_map/store_results/pallas_call | solution.py:307
Async XLA Ops:
  19.4 0.8 %copy-start = (f32[128,1024]{1,0:T(8,128)}, f32[128,1024]{1,0:T(8,128)S(1)}, u32[]{:S(2)}) copy-start(f32[128,1024]{1,0:T(8,128)S(1)} %get-tuple-element.4.resist) | copy-start | bytes 1572868
  20.2 0.8 %copy-start.1 = (f32[128,1024]{1,0:T(8,128)}, f32[128,1024]{1,0:T(8,128)S(1)}, u32[]{:S(2)}) copy-start(f32[128,1024]{1,0:T(8,128)S(1)} %get-tuple-element.5.grad) | copy-start | bytes 1572868

commit v4 on v3

--- a/solution.py
+++ b/solution.py
@@ -307,11 +307,11 @@
     return pl.pallas_call(
         store,
         out_shape=(out, out),
-        in_specs=[anywhere, anywhere],
+        in_specs=[in_vmem, in_vmem],
         out_specs=(anywhere, anywhere),
         scratch_shapes=[pltpu.SemaphoreType.DMA((2,))],
         name="store_results",
-    )(resist, grad)
+    )(*[pltpu.with_memory_space_constraint(x, pltpu.VMEM) for x in (resist, grad)])
 
 
 def solution(mesh):

time: 54.1 us -> 20.6 us (0.38)
  Pallas kernels: 51.7 us -> 19.8 us
  local copies, waits for them, and re-layouts: 1.58 us -> 0 us
    pallas_call x1, Pallas kernels: 32.9 us -> 0.99 us  [shards(): pl.pallas_call(store, out_shape=(out, out), in_specs=[in_vmem, in_vmem],...]
    unnamed x4 -> x0, local copies, waits for them, and re-layouts: 1.58 us -> none
where the time goes in v4:
time: 20.6 us; the launch traced here: 20.4 us
  Pallas kernels  19.8 us (96%)
  between operations  0.64 us (3%)
    pallas_call x1, Pallas kernels, shards(): pl.pallas_call(functools.partial(kernel, count, names), out_shape=(held,...  18.8 us
    pallas_call x1, Pallas kernels, shards(): pl.pallas_call(store, out_shape=(out, out), in_specs=[in_vmem, in_vmem],...  0.99 us

profile of v4, /device:TPU:0, one launch (start us, length us, event | category | flops | bytes accessed | tf_op | source)
XLA Modules:
  0.0 20.4 jit_solution(6006900534262313178)
XLA Ops:
  0.6 18.8 %litho_step.1 = (f32[128,1024]{1,0:T(8,128)S(1)}, f32[128,1024]{1,0:T(8,128)S(1)}) custom-call(f32[16]{0:T(128)} %weights_ref.1, f32[128,1024]{1,0:T(8,128)} %mask_hbm.1, s32[128,1024]{1,0:T(8,128)} %target_hbm.1, f32[2,16,32,128]{3,2,1,0:T(8,128)} %spectra_hbm.1, bf16[2,1024,256]{2,1,0:T(8,128)(2,1)} %constant.26.clone.refs_0_, ...), custom_call_target="tpu_custom_call" | custom-call | tf_op jit(solution)/shard_map/litho_step/pallas_call | solution.py:282
  19.4 1.0 %store_results.1 = (f32[128,1024]{1,0:T(8,128)}, f32[128,1024]{1,0:T(8,128)}) custom-call(f32[128,1024]{1,0:T(8,128)S(1)} %get-tuple-element.4.resist, f32[128,1024]{1,0:T(8,128)S(1)} %get-tuple-element.5.grad), custom_call_target="tpu_custom_call" | custom-call | tf_op jit(solution)/shard_map/store_results/pallas_call | solution.py:307

commit v5 on v4

--- a/solution.py
+++ b/solution.py
@@ -13,7 +13,7 @@
 MARGIN = 64
 STEEPNESS = 8.0
 THRESHOLD = 0.35
-GROUP = 4
+GROUP = 16
 MESH = pl.DeviceIdType.MESH
 
 
@@ -26,6 +26,18 @@
 def deep_table(table):
     high, low = split_table(table)
     return np.concatenate([high, high, low], axis=1)
+
+
+def tall_table(table):
+    high, low = split_table(table)
+    return np.concatenate(
+        [np.concatenate([high, high], axis=1), np.concatenate([low, low], axis=1)], axis=0
+    )
+
+
+def long_table(table):
+    high, low = split_table(table)
+    return np.concatenate([high, high, low], axis=0)
 
 
 def cos_sin(frequencies, positions):
@@ -73,14 +85,14 @@
     return {
         "forward": np.stack(split_table(forward)),
         "rows_in": deep_table(rows_in),
-        "inverse": np.stack(split_table(inverse)),
+        "inverse": long_table(inverse),
         "rows_out": deep_table(rows_out),
         "up_cols": np.stack(split_table(up_cols)),
         "up_rows": deep_table(up_rows),
-        "down_rows": deep_table(up_rows.T),
+        "down_rows": tall_table(up_rows.T),
         "down_cols": np.stack(split_table(up_cols.T)),
-        "rows_back": deep_table(rows_out.T),
-        "inverse_back": np.stack(split_table(inverse.T)),
+        "rows_back": tall_table(rows_out.T),
+        "inverse_back": long_table(inverse.T),
         "rows_own": deep_table(own.T),
         "rows_near": deep_table(rows_near),
         "forward_back": np.stack(split_table(forward.T)),
@@ -107,6 +119,17 @@
 def table_times(deep, values):
     high, low = split(values)
     return dot(deep, jnp.concatenate([high, low, high], axis=0))
+
+
+def times_long(values, long):
+    high, low = split(values)
+    return dot(jnp.concatenate([high, low, high], axis=1), long)
+
+
+def tall_times(tall, values):
+    product = dot(tall, jnp.concatenate(split(values), axis=0))
+    half = product.shape[0] // 2
+    return product[:half] + product[half:]
 
 
 def fold(product):
@@ -211,7 +234,7 @@
             real = spectra[0, k] * spec_real - spectra[1, k] * spec_imag
             imag = spectra[0, k] * spec_imag + spectra[1, k] * spec_real
             blocks.append(jnp.concatenate([real, imag], axis=1))
-        across = times_table(jnp.concatenate(blocks, axis=0), inverse)
+        across = times_long(jnp.concatenate(blocks, axis=0), inverse[...])
         half = across.shape[1] // 2
         for place, k in enumerate(members):
             part = across[place * freq_rows : (place + 1) * freq_rows]
@@ -226,7 +249,7 @@
     resist[...] = image
     loads["target"].wait()
     slopes = (4.0 * STEEPNESS) * (image - target[...].astype(jnp.float32)) * image * (1.0 - image)
-    slopes = times_table(table_times(table("down_rows")[...], slopes), table("down_cols"))
+    slopes = times_table(tall_times(table("down_rows")[...], slopes), table("down_cols"))
     slopes = jnp.concatenate([slopes, slopes], axis=0)
 
     rows_back, inverse_back = table("rows_back"), table("inverse_back")
@@ -235,9 +258,9 @@
         members = range(first, min(first + GROUP, kernels))
         blocks = []
         for k in members:
-            part = table_times(rows_back[...], fields[k] * slopes)
+            part = tall_times(rows_back[...], fields[k] * slopes)
             blocks.append(jnp.concatenate([part[:freq_rows], part[freq_rows:]], axis=1))
-        across = times_table(jnp.concatenate(blocks, axis=0), inverse_back)
+        across = times_long(jnp.concatenate(blocks, axis=0), inverse_back[...])
         for place, k in enumerate(members):
             part = across[place * freq_rows : (place + 1) * freq_rows]
             real, imag = part[:, :freq_cols], part[:, freq_cols:]

time: 20.6 us -> 20.4 us (level)
  no operation moved by 1% of the time
where the time goes in v5:
time: 20.4 us; the launch traced here: 20.3 us
  Pallas kernels  19.7 us (97%)
  between operations  0.64 us (3%)
    pallas_call x1, Pallas kernels, shards(): pl.pallas_call(functools.partial(kernel, count, names), out_shape=(held,...  18.7 us
    pallas_call x1, Pallas kernels, shards(): pl.pallas_call(store, out_shape=(out, out), in_specs=[in_vmem, in_vmem],...  0.99 us

profile of v5, /device:TPU:0, one launch (start us, length us, event | category | flops | bytes accessed | tf_op | source)
XLA Modules:
  0.0 20.3 jit_solution(5739034644489782357)
XLA Ops:
  0.6 18.7 %litho_step.1 = (f32[128,1024]{1,0:T(8,128)S(1)}, f32[128,1024]{1,0:T(8,128)S(1)}) custom-call(f32[16]{0:T(128)} %weights_ref.1, f32[128,1024]{1,0:T(8,128)} %mask_hbm.1, s32[128,1024]{1,0:T(8,128)} %target_hbm.1, f32[2,16,32,128]{3,2,1,0:T(8,128)} %spectra_hbm.1, bf16[2,1024,256]{2,1,0:T(8,128)(2,1)} %constant.26.clone.refs_0_, ...), custom_call_target="tpu_custom_call" | custom-call | tf_op jit(solution)/shard_map/litho_step/pallas_call | solution.py:305
  19.3 1.0 %store_results.1 = (f32[128,1024]{1,0:T(8,128)}, f32[128,1024]{1,0:T(8,128)}) custom-call(f32[128,1024]{1,0:T(8,128)S(1)} %get-tuple-element.4.resist, f32[128,1024]{1,0:T(8,128)S(1)} %get-tuple-element.5.grad), custom_call_target="tpu_custom_call" | custom-call | tf_op jit(solution)/shard_map/store_results/pallas_call | solution.py:330

commit v6 on v5

--- a/solution.py
+++ b/solution.py
@@ -14,6 +14,7 @@
 STEEPNESS = 8.0
 THRESHOLD = 0.35
 GROUP = 16
+CHUNKS = 4
 MESH = pl.DeviceIdType.MESH
 
 
@@ -109,11 +110,11 @@
     return jnp.dot(left, right, preferred_element_type=jnp.float32)
 
 
-def times_table(values, table):
+def times_table(values, table, part=slice(None)):
     rows = values.shape[0]
     high, low = split(values)
-    both = dot(jnp.concatenate([high, low], axis=0), table[0])
-    return both[:rows] + (both[rows:] + dot(high, table[1]))
+    both = dot(jnp.concatenate([high, low], axis=0), table[0, part])
+    return both[:rows] + (both[rows:] + dot(high, table[1, part]))
 
 
 def table_times(deep, values):
@@ -164,21 +165,26 @@
     for other in (previous, following):
         pl.semaphore_signal(barrier, inc=1, device_id={"tiles": other}, device_id_type=MESH)
 
-    sources = {"mask": (mask_hbm, mask), "spectra": (spectra_hbm, spectra), "target": (target_hbm, target)}
+    sources = {"spectra": (spectra_hbm, spectra), "target": (target_hbm, target)}
     for name, source in zip(names, tables_hbm):
         sources[name] = (source, tables[name])
-    order = ["mask", "forward", "rows_in", "spectra", "inverse", "rows_out", "up_cols",
-             "up_rows", "target", "down_rows", "down_cols", "rows_back", "inverse_back",
-             "rows_own", "rows_near", "forward_back"]
+    columns = mask.shape[1]
+    chunks = CHUNKS if columns % (128 * CHUNKS) == 0 else 1
+    parts = [pl.ds(at * (columns // chunks), columns // chunks) for at in range(chunks)]
     loads = {}
-    for at, name in enumerate(order):
-        loads[name] = pltpu.make_async_copy(*sources[name], in_sem.at[at])
-    for name in order[:4]:
+
+    def load(name, source, destination):
+        loads[name] = pltpu.make_async_copy(source, destination, in_sem.at[len(loads)])
         loads[name].start()
 
     def table(name):
         loads[name].wait()
         return tables[name]
+
+    for at, part in enumerate(parts):
+        load(("mask", at), mask_hbm.at[:, part], mask.at[:, part])
+        load(("forward", at), sources["forward"][0].at[:, part], tables["forward"].at[:, part])
+    load("rows_in", *sources["rows_in"])
 
     def swap(step, to_previous, to_following):
         landed = recv1 if step == 0 else recv2
@@ -196,18 +202,25 @@
             copy.start()
         return copies
 
-    loads["mask"].wait()
-    transmit[...] = jnp.tanh(mask[...])
-    forward = table("forward")
-    for name in order[4:]:
-        loads[name].start()
-    column_spec = times_table(transmit[...], forward)
+    later = ("spectra", "inverse", "rows_out", "up_cols", "up_rows", "target", "down_rows",
+             "down_cols", "rows_back", "inverse_back", "rows_own", "rows_near", "forward_back")
+
+    column_spec = None
+    for at, part in enumerate(parts):
+        loads["mask", at].wait()
+        transmit[:, part] = jnp.tanh(mask[:, part])
+        loads["forward", at].wait()
+        if at == len(parts) - 1:
+            for name in later:
+                load(name, *sources[name])
+        term = times_table(transmit[:, part], tables["forward"], part)
+        column_spec = term if column_spec is None else column_spec + term
     product = table_times(table("rows_in")[...], column_spec)
     span = product.shape[0] // 3
     send1[0] = fold(product[:span])
     send1[1] = fold(product[span : 2 * span])
     pl.semaphore_wait(barrier, 2)
-    copies = swap(0, send1.at[0], send1.at[1])
+    first_swap = swap(0, send1.at[0], send1.at[1])
     own_spec = fold(product[2 * span :])
 
     kernels, freq_rows, freq_cols = spectra.shape[1:]
@@ -220,8 +233,8 @@
         spectra[1, k] = spectra[1, k] * scale
     inverse, rows_out = table("inverse"), table("rows_out")
 
-    for copy in copies:
-        copy.wait()
+    for copy in first_swap:
+        copy.wait_recv()
     spec = own_spec + (recv1[0] + recv1[1])
     spec_real, spec_imag = spec[:, :freq_cols], spec[:, freq_cols:]
 
@@ -270,15 +283,17 @@
             grad_imag = term_imag if grad_imag is None else grad_imag + term_imag
     window_grad = jnp.concatenate([grad_real, grad_imag], axis=1)
     send2[...] = window_grad
-    copies = swap(1, send2, send2)
+    second_swap = swap(1, send2, send2)
     merged = table_times(table("rows_own")[...], unfold(window_grad))
     rows_near, forward_back = table("rows_near"), table("forward_back")
-    for copy in copies:
-        copy.wait()
+    for copy in second_swap:
+        copy.wait_recv()
     near = jnp.concatenate([unfold(recv2[0]), unfold(recv2[1])], axis=0)
     merged = merged + table_times(rows_near[...], near)
     held = transmit[...]
     grad[...] = times_table(merged, forward_back) * (1.0 - held * held)
+    for copy in first_swap + second_swap:
+        copy.wait_send()
 
 
 def store(resist, grad, resist_hbm, grad_hbm, sems):
@@ -318,7 +333,7 @@
             pltpu.VMEM((2,) + spectrum, jnp.float32),
             pltpu.VMEM(spectrum, jnp.float32),
             pltpu.VMEM((2,) + spectrum, jnp.float32),
-            pltpu.SemaphoreType.DMA((3 + len(names),)),
+            pltpu.SemaphoreType.DMA((2 + 2 * CHUNKS + len(names),)),
             pltpu.SemaphoreType.DMA((4,)),
             pltpu.SemaphoreType.DMA((4,)),
         ],

time: 20.4 us -> 20.5 us (level)
  no operation moved by 1% of the time
where the time goes in v6:
time: 20.5 us; the launch traced here: 20.4 us
  Pallas kernels  19.7 us (96%)
  between operations  0.64 us (3%)
    pallas_call x1, Pallas kernels, shards(): pl.pallas_call(functools.partial(kernel, count, names), out_shape=(held,...  18.7 us
    pallas_call x1, Pallas kernels, shards(): pl.pallas_call(store, out_shape=(out, out), in_specs=[in_vmem, in_vmem],...  0.99 us

profile of v6, /device:TPU:0, one launch (start us, length us, event | category | flops | bytes accessed | tf_op | source)
XLA Modules:
  0.0 20.4 jit_solution(4761481992133908664)
XLA Ops:
  0.6 18.7 %litho_step.1 = (f32[128,1024]{1,0:T(8,128)S(1)}, f32[128,1024]{1,0:T(8,128)S(1)}) custom-call(f32[16]{0:T(128)} %weights_ref.1, f32[128,1024]{1,0:T(8,128)} %mask_hbm.1, s32[128,1024]{1,0:T(8,128)} %target_hbm.1, f32[2,16,32,128]{3,2,1,0:T(8,128)} %spectra_hbm.1, bf16[2,1024,256]{2,1,0:T(8,128)(2,1)} %constant.26.clone.refs_0_, ...), custom_call_target="tpu_custom_call" | custom-call | tf_op jit(solution)/shard_map/litho_step/pallas_call | solution.py:320
  19.4 1.0 %store_results.1 = (f32[128,1024]{1,0:T(8,128)}, f32[128,1024]{1,0:T(8,128)}) custom-call(f32[128,1024]{1,0:T(8,128)S(1)} %get-tuple-element.4.resist, f32[128,1024]{1,0:T(8,128)S(1)} %get-tuple-element.5.grad), custom_call_target="tpu_custom_call" | custom-call | tf_op jit(solution)/shard_map/store_results/pallas_call | solution.py:345

commit v7 on v6

--- a/solution.py
+++ b/solution.py
@@ -13,7 +13,7 @@
 MARGIN = 64
 STEEPNESS = 8.0
 THRESHOLD = 0.35
-GROUP = 16
+GROUP = 4
 CHUNKS = 4
 MESH = pl.DeviceIdType.MESH
 
@@ -239,22 +239,24 @@
     spec_real, spec_imag = spec[:, :freq_cols], spec[:, freq_cols:]
 
     coarse = fields.shape[1] // 2
+    width = fields.shape[2] // GROUP
+    blocks = []
+    for k in range(kernels):
+        real = spectra[0, k] * spec_real - spectra[1, k] * spec_imag
+        imag = spectra[0, k] * spec_imag + spectra[1, k] * spec_real
+        blocks.append(jnp.concatenate([real, imag], axis=1))
+    across = times_long(jnp.concatenate(blocks, axis=0), inverse[...])
     power = None
-    for first in range(0, kernels, GROUP):
-        members = range(first, min(first + GROUP, kernels))
+    for group in range(fields.shape[0]):
         blocks = []
-        for k in members:
-            real = spectra[0, k] * spec_real - spectra[1, k] * spec_imag
-            imag = spectra[0, k] * spec_imag + spectra[1, k] * spec_real
-            blocks.append(jnp.concatenate([real, imag], axis=1))
-        across = times_long(jnp.concatenate(blocks, axis=0), inverse[...])
-        half = across.shape[1] // 2
-        for place, k in enumerate(members):
-            part = across[place * freq_rows : (place + 1) * freq_rows]
-            part = jnp.concatenate([part[:, :half], part[:, half:]], axis=0)
-            field = table_times(rows_out[...], part)
-            fields[k] = field
-            term = field[:coarse] * field[:coarse] + field[coarse:] * field[coarse:]
+        for k in range(group * GROUP, (group + 1) * GROUP):
+            part = across[k * freq_rows : (k + 1) * freq_rows]
+            blocks.append(jnp.concatenate([part[:, :width], part[:, width:]], axis=0))
+        field = table_times(rows_out[...], jnp.concatenate(blocks, axis=1))
+        fields[group] = field
+        terms = field[:coarse] * field[:coarse] + field[coarse:] * field[coarse:]
+        for place in range(GROUP):
+            term = terms[:, place * width : (place + 1) * width]
             power = term if power is None else power + term
 
     intensity = table_times(table("up_rows")[...], times_table(power, table("up_cols")))
@@ -264,23 +266,24 @@
     slopes = (4.0 * STEEPNESS) * (image - target[...].astype(jnp.float32)) * image * (1.0 - image)
     slopes = times_table(tall_times(table("down_rows")[...], slopes), table("down_cols"))
     slopes = jnp.concatenate([slopes, slopes], axis=0)
+    slopes = jnp.concatenate([slopes] * GROUP, axis=1)
 
     rows_back, inverse_back = table("rows_back"), table("inverse_back")
+    blocks = []
+    for group in range(fields.shape[0]):
+        part = tall_times(rows_back[...], fields[group] * slopes)
+        for place in range(GROUP):
+            piece = part[:, place * width : (place + 1) * width]
+            blocks.append(jnp.concatenate([piece[:freq_rows], piece[freq_rows:]], axis=1))
+    across = times_long(jnp.concatenate(blocks, axis=0), inverse_back[...])
     grad_real = grad_imag = None
-    for first in range(0, kernels, GROUP):
-        members = range(first, min(first + GROUP, kernels))
-        blocks = []
-        for k in members:
-            part = tall_times(rows_back[...], fields[k] * slopes)
-            blocks.append(jnp.concatenate([part[:freq_rows], part[freq_rows:]], axis=1))
-        across = times_long(jnp.concatenate(blocks, axis=0), inverse_back[...])
-        for place, k in enumerate(members):
-            part = across[place * freq_rows : (place + 1) * freq_rows]
-            real, imag = part[:, :freq_cols], part[:, freq_cols:]
-            term_real = real * spectra[0, k] + imag * spectra[1, k]
-            term_imag = imag * spectra[0, k] - real * spectra[1, k]
-            grad_real = term_real if grad_real is None else grad_real + term_real
-            grad_imag = term_imag if grad_imag is None else grad_imag + term_imag
+    for k in range(kernels):
+        part = across[k * freq_rows : (k + 1) * freq_rows]
+        real, imag = part[:, :freq_cols], part[:, freq_cols:]
+        term_real = real * spectra[0, k] + imag * spectra[1, k]
+        term_imag = imag * spectra[0, k] - real * spectra[1, k]
+        grad_real = term_real if grad_real is None else grad_real + term_real
+        grad_imag = term_imag if grad_imag is None else grad_imag + term_imag
     window_grad = jnp.concatenate([grad_real, grad_imag], axis=1)
     send2[...] = window_grad
     second_swap = swap(1, send2, send2)
@@ -328,7 +331,7 @@
             pltpu.VMEM((strip_rows, columns), jnp.int32),
             pltpu.VMEM(kernel_spectra.shape, jnp.float32),
             pltpu.VMEM((strip_rows, columns), jnp.float32),
-            pltpu.VMEM((kernels, 4 * freq_rows, 2 * freq_cols), jnp.float32),
+            pltpu.VMEM((kernels // GROUP, 4 * freq_rows, GROUP * 2 * freq_cols), jnp.float32),
             pltpu.VMEM((2,) + spectrum, jnp.float32),
             pltpu.VMEM((2,) + spectrum, jnp.float32),
             pltpu.VMEM(spectrum, jnp.float32),

time: 20.5 us -> 20.5 us (level)
  no operation moved by 1% of the time
where the time goes in v7:
time: 20.5 us; the launch traced here: 20.4 us
  Pallas kernels  19.7 us (96%)
  between operations  0.64 us (3%)
    pallas_call x1, Pallas kernels, shards(): pl.pallas_call(functools.partial(kernel, count, names), out_shape=(held,...  18.7 us
    pallas_call x1, Pallas kernels, shards(): pl.pallas_call(store, out_shape=(out, out), in_specs=[in_vmem, in_vmem],...  0.99 us

profile of v7, /device:TPU:0, one launch (start us, length us, event | category | flops | bytes accessed | tf_op | source)
XLA Modules:
  0.0 20.4 jit_solution(11041445913741059919)
XLA Ops:
  0.6 18.7 %litho_step.1 = (f32[128,1024]{1,0:T(8,128)S(1)}, f32[128,1024]{1,0:T(8,128)S(1)}) custom-call(f32[16]{0:T(128)} %weights_ref.1, f32[128,1024]{1,0:T(8,128)} %mask_hbm.1, s32[128,1024]{1,0:T(8,128)} %target_hbm.1, f32[2,16,32,128]{3,2,1,0:T(8,128)} %spectra_hbm.1, bf16[2,1024,256]{2,1,0:T(8,128)(2,1)} %constant.26.clone.refs_0_, ...), custom_call_target="tpu_custom_call" | custom-call | tf_op jit(solution)/shard_map/litho_step/pallas_call | solution.py:323
  19.4 1.0 %store_results.1 = (f32[128,1024]{1,0:T(8,128)}, f32[128,1024]{1,0:T(8,128)}) custom-call(f32[128,1024]{1,0:T(8,128)S(1)} %get-tuple-element.4.resist, f32[128,1024]{1,0:T(8,128)S(1)} %get-tuple-element.5.grad), custom_call_target="tpu_custom_call" | custom-call | tf_op jit(solution)/shard_map/store_results/pallas_call | solution.py:348

commit v8 on v7

--- a/solution.py
+++ b/solution.py
@@ -34,11 +34,6 @@
     return np.concatenate(
         [np.concatenate([high, high], axis=1), np.concatenate([low, low], axis=1)], axis=0
     )
-
-
-def long_table(table):
-    high, low = split_table(table)
-    return np.concatenate([high, high, low], axis=0)
 
 
 def cos_sin(frequencies, positions):
@@ -86,17 +81,14 @@
     return {
         "forward": np.stack(split_table(forward)),
         "rows_in": deep_table(rows_in),
-        "inverse": long_table(inverse),
+        "inverse": np.stack(split_table(inverse)),
         "rows_out": deep_table(rows_out),
         "up_cols": np.stack(split_table(up_cols)),
         "up_rows": deep_table(up_rows),
         "down_rows": tall_table(up_rows.T),
-        "down_cols": np.stack(split_table(up_cols.T)),
         "rows_back": tall_table(rows_out.T),
-        "inverse_back": long_table(inverse.T),
         "rows_own": deep_table(own.T),
         "rows_near": deep_table(rows_near),
-        "forward_back": np.stack(split_table(forward.T)),
     }
 
 
@@ -110,21 +102,22 @@
     return jnp.dot(left, right, preferred_element_type=jnp.float32)
 
 
-def times_table(values, table, part=slice(None)):
+def dot_across(left, right):
+    return lax.dot_general(
+        left, right, (((1,), (1,)), ((), ())), preferred_element_type=jnp.float32
+    )
+
+
+def times_table(values, table, part=slice(None), product=dot):
     rows = values.shape[0]
     high, low = split(values)
-    both = dot(jnp.concatenate([high, low], axis=0), table[0, part])
-    return both[:rows] + (both[rows:] + dot(high, table[1, part]))
+    both = product(jnp.concatenate([high, low], axis=0), table[0, part])
+    return both[:rows] + (both[rows:] + product(high, table[1, part]))
 
 
 def table_times(deep, values):
     high, low = split(values)
     return dot(deep, jnp.concatenate([high, low, high], axis=0))
-
-
-def times_long(values, long):
-    high, low = split(values)
-    return dot(jnp.concatenate([high, low, high], axis=1), long)
 
 
 def tall_times(tall, values):
@@ -203,7 +196,7 @@
         return copies
 
     later = ("spectra", "inverse", "rows_out", "up_cols", "up_rows", "target", "down_rows",
-             "down_cols", "rows_back", "inverse_back", "rows_own", "rows_near", "forward_back")
+             "rows_back", "rows_own", "rows_near")
 
     column_spec = None
     for at, part in enumerate(parts):
@@ -245,7 +238,7 @@
         real = spectra[0, k] * spec_real - spectra[1, k] * spec_imag
         imag = spectra[0, k] * spec_imag + spectra[1, k] * spec_real
         blocks.append(jnp.concatenate([real, imag], axis=1))
-    across = times_long(jnp.concatenate(blocks, axis=0), inverse[...])
+    across = times_table(jnp.concatenate(blocks, axis=0), inverse)
     power = None
     for group in range(fields.shape[0]):
         blocks = []
@@ -264,18 +257,19 @@
     resist[...] = image
     loads["target"].wait()
     slopes = (4.0 * STEEPNESS) * (image - target[...].astype(jnp.float32)) * image * (1.0 - image)
-    slopes = times_table(tall_times(table("down_rows")[...], slopes), table("down_cols"))
+    slopes = tall_times(table("down_rows")[...], slopes)
+    slopes = times_table(slopes, tables["up_cols"], product=dot_across)
     slopes = jnp.concatenate([slopes, slopes], axis=0)
     slopes = jnp.concatenate([slopes] * GROUP, axis=1)
 
-    rows_back, inverse_back = table("rows_back"), table("inverse_back")
+    rows_back = table("rows_back")
     blocks = []
     for group in range(fields.shape[0]):
         part = tall_times(rows_back[...], fields[group] * slopes)
         for place in range(GROUP):
             piece = part[:, place * width : (place + 1) * width]
             blocks.append(jnp.concatenate([piece[:freq_rows], piece[freq_rows:]], axis=1))
-    across = times_long(jnp.concatenate(blocks, axis=0), inverse_back[...])
+    across = times_table(jnp.concatenate(blocks, axis=0), inverse, product=dot_across)
     grad_real = grad_imag = None
     for k in range(kernels):
         part = across[k * freq_rows : (k + 1) * freq_rows]
@@ -288,13 +282,13 @@
     send2[...] = window_grad
     second_swap = swap(1, send2, send2)
     merged = table_times(table("rows_own")[...], unfold(window_grad))
-    rows_near, forward_back = table("rows_near"), table("forward_back")
+    rows_near = table("rows_near")
     for copy in second_swap:
         copy.wait_recv()
     near = jnp.concatenate([unfold(recv2[0]), unfold(recv2[1])], axis=0)
     merged = merged + table_times(rows_near[...], near)
     held = transmit[...]
-    grad[...] = times_table(merged, forward_back) * (1.0 - held * held)
+    grad[...] = times_table(merged, tables["forward"], product=dot_across) * (1.0 - held * held)
     for copy in first_swap + second_swap:
         copy.wait_send()
 

time: 20.5 us -> 21.1 us (1.029)
  Pallas kernels: 19.7 us -> 20.4 us
    pallas_call x1, Pallas kernels: 18.7 us -> 19.4 us  [shards(): pl.pallas_call(functools.partial(kernel, count, names), out_shape=(held,...]
where the time goes in v8:
time: 21.1 us; the launch traced here: 21 us
  Pallas kernels  20.4 us (97%)
  between operations  0.64 us (3%)
    pallas_call x1, Pallas kernels, shards(): pl.pallas_call(functools.partial(kernel, count, names), out_shape=(held,...  19.4 us
    pallas_call x1, Pallas kernels, shards(): pl.pallas_call(store, out_shape=(out, out), in_specs=[in_vmem, in_vmem],...  0.99 us

profile of v8, /device:TPU:0, one launch (start us, length us, event | category | flops | bytes accessed | tf_op | source)
XLA Modules:
  0.0 21.0 jit_solution(10406265285579910938)
XLA Ops:
  0.6 19.4 %litho_step.1 = (f32[128,1024]{1,0:T(8,128)S(1)}, f32[128,1024]{1,0:T(8,128)S(1)}) custom-call(f32[16]{0:T(128)} %weights_ref.1, f32[128,1024]{1,0:T(8,128)} %mask_hbm.1, s32[128,1024]{1,0:T(8,128)} %target_hbm.1, f32[2,16,32,128]{3,2,1,0:T(8,128)} %spectra_hbm.1, bf16[2,1024,256]{2,1,0:T(8,128)(2,1)} %constant.20.clone.refs_0_, ...), custom_call_target="tpu_custom_call" | custom-call | tf_op jit(solution)/shard_map/litho_step/pallas_call | solution.py:317
  20.0 1.0 %store_results.1 = (f32[128,1024]{1,0:T(8,128)}, f32[128,1024]{1,0:T(8,128)}) custom-call(f32[128,1024]{1,0:T(8,128)S(1)} %get-tuple-element.4.resist, f32[128,1024]{1,0:T(8,128)S(1)} %get-tuple-element.5.grad), custom_call_target="tpu_custom_call" | custom-call | tf_op jit(solution)/shard_map/store_results/pallas_call | solution.py:342

commit v9 on v7

--- a/solution.py
+++ b/solution.py
@@ -240,24 +240,28 @@
 
     coarse = fields.shape[1] // 2
     width = fields.shape[2] // GROUP
-    blocks = []
-    for k in range(kernels):
-        real = spectra[0, k] * spec_real - spectra[1, k] * spec_imag
-        imag = spectra[0, k] * spec_imag + spectra[1, k] * spec_real
-        blocks.append(jnp.concatenate([real, imag], axis=1))
-    across = times_long(jnp.concatenate(blocks, axis=0), inverse[...])
-    power = None
-    for group in range(fields.shape[0]):
+
+    def add_fields(group, power):
         blocks = []
-        for k in range(group * GROUP, (group + 1) * GROUP):
-            part = across[k * freq_rows : (k + 1) * freq_rows]
+        for place in range(GROUP):
+            k = group * GROUP + place
+            real = spectra[0, k] * spec_real - spectra[1, k] * spec_imag
+            imag = spectra[0, k] * spec_imag + spectra[1, k] * spec_real
+            blocks.append(jnp.concatenate([real, imag], axis=1))
+        across = times_long(jnp.concatenate(blocks, axis=0), inverse[...])
+        blocks = []
+        for place in range(GROUP):
+            part = across[place * freq_rows : (place + 1) * freq_rows]
             blocks.append(jnp.concatenate([part[:, :width], part[:, width:]], axis=0))
         field = table_times(rows_out[...], jnp.concatenate(blocks, axis=1))
         fields[group] = field
         terms = field[:coarse] * field[:coarse] + field[coarse:] * field[coarse:]
         for place in range(GROUP):
-            term = terms[:, place * width : (place + 1) * width]
-            power = term if power is None else power + term
+            power = power + terms[:, place * width : (place + 1) * width]
+        return power
+
+    groups = fields.shape[0]
+    power = lax.fori_loop(0, groups, add_fields, jnp.zeros((coarse, width), jnp.float32))
 
     intensity = table_times(table("up_rows")[...], times_table(power, table("up_cols")))
     image = jax.nn.sigmoid(STEEPNESS * (intensity - THRESHOLD))
@@ -269,21 +273,25 @@
     slopes = jnp.concatenate([slopes] * GROUP, axis=1)
 
     rows_back, inverse_back = table("rows_back"), table("inverse_back")
-    blocks = []
-    for group in range(fields.shape[0]):
+
+    def add_gradient(group, sums):
+        grad_real, grad_imag = sums
         part = tall_times(rows_back[...], fields[group] * slopes)
+        blocks = []
         for place in range(GROUP):
             piece = part[:, place * width : (place + 1) * width]
             blocks.append(jnp.concatenate([piece[:freq_rows], piece[freq_rows:]], axis=1))
-    across = times_long(jnp.concatenate(blocks, axis=0), inverse_back[...])
-    grad_real = grad_imag = None
-    for k in range(kernels):
-        part = across[k * freq_rows : (k + 1) * freq_rows]
-        real, imag = part[:, :freq_cols], part[:, freq_cols:]
-        term_real = real * spectra[0, k] + imag * spectra[1, k]
-        term_imag = imag * spectra[0, k] - real * spectra[1, k]
-        grad_real = term_real if grad_real is None else grad_real + term_real
-        grad_imag = term_imag if grad_imag is None else grad_imag + term_imag
+        across = times_long(jnp.concatenate(blocks, axis=0), inverse_back[...])
+        for place in range(GROUP):
+            k = group * GROUP + place
+            part = across[place * freq_rows : (place + 1) * freq_rows]
+            real, imag = part[:, :freq_cols], part[:, freq_cols:]
+            grad_real = grad_real + (real * spectra[0, k] + imag * spectra[1, k])
+            grad_imag = grad_imag + (imag * spectra[0, k] - real * spectra[1, k])
+        return grad_real, grad_imag
+
+    empty = jnp.zeros((freq_rows, freq_cols), jnp.float32)
+    grad_real, grad_imag = lax.fori_loop(0, groups, add_gradient, (empty, empty))
     window_grad = jnp.concatenate([grad_real, grad_imag], axis=1)
     send2[...] = window_grad
     second_swap = swap(1, send2, send2)

time: 20.5 us -> 22 us (1.073)
  Pallas kernels: 19.7 us -> 21.2 us
    pallas_call x1, Pallas kernels: 18.7 us -> 20.2 us  [shards(): pl.pallas_call(functools.partial(kernel, count, names), out_shape=(held,...]
where the time goes in v9:
time: 22 us; the launch traced here: 21.8 us
  Pallas kernels  21.2 us (96%)
  between operations  0.64 us (3%)
    pallas_call x1, Pallas kernels, shards(): pl.pallas_call(functools.partial(kernel, count, names), out_shape=(held,...  20.2 us
    pallas_call x1, Pallas kernels, shards(): pl.pallas_call(store, out_shape=(out, out), in_specs=[in_vmem, in_vmem],...  0.99 us

profile of v9, /device:TPU:0, one launch (start us, length us, event | category | flops | bytes accessed | tf_op | source)
XLA Modules:
  0.0 21.8 jit_solution(3070460513199887848)
XLA Ops:
  0.6 20.2 %litho_step.1 = (f32[128,1024]{1,0:T(8,128)S(1)}, f32[128,1024]{1,0:T(8,128)S(1)}) custom-call(f32[16]{0:T(128)} %weights_ref.1, f32[128,1024]{1,0:T(8,128)} %mask_hbm.1, s32[128,1024]{1,0:T(8,128)} %target_hbm.1, f32[2,16,32,128]{3,2,1,0:T(8,128)} %spectra_hbm.1, bf16[2,1024,256]{2,1,0:T(8,128)(2,1)} %constant.26.clone.refs_0_, ...), custom_call_target="tpu_custom_call" | custom-call | tf_op jit(solution)/shard_map/litho_step/pallas_call | solution.py:331
  20.9 1.0 %store_results.1 = (f32[128,1024]{1,0:T(8,128)}, f32[128,1024]{1,0:T(8,128)}) custom-call(f32[128,1024]{1,0:T(8,128)S(1)} %get-tuple-element.4.resist, f32[128,1024]{1,0:T(8,128)S(1)} %get-tuple-element.5.grad), custom_call_target="tpu_custom_call" | custom-call | tf_op jit(solution)/shard_map/store_results/pallas_call | solution.py:356

commit v10 on v7

--- a/solution.py
+++ b/solution.py
@@ -151,11 +151,12 @@
 def kernel(count, names, weights_ref, mask_hbm, target_hbm, spectra_hbm, *refs):
     tables_hbm = refs[: len(names)]
     refs = refs[len(names) :]
-    resist, grad = refs[:2]
-    refs = refs[2:]
-    tables = dict(zip(names, refs[: len(names)]))
-    refs = refs[len(names) :]
-    (mask, target, spectra, transmit, fields,
+    resist, merged_ref, transmit, last_table = refs[:4]
+    refs = refs[4:]
+    held = [name for name in names if name != "forward_back"]
+    tables = dict(zip(held, refs[: len(held)]), forward_back=last_table)
+    refs = refs[len(held) :]
+    (mask, target, spectra, fields,
      send1, recv1, send2, recv2, in_sem, send_sem, recv_sem) = refs
 
     me = lax.axis_index("tiles")
@@ -288,24 +289,32 @@
     send2[...] = window_grad
     second_swap = swap(1, send2, send2)
     merged = table_times(table("rows_own")[...], unfold(window_grad))
-    rows_near, forward_back = table("rows_near"), table("forward_back")
+    rows_near = table("rows_near")
+    loads["forward_back"].wait()
     for copy in second_swap:
         copy.wait_recv()
     near = jnp.concatenate([unfold(recv2[0]), unfold(recv2[1])], axis=0)
-    merged = merged + table_times(rows_near[...], near)
-    held = transmit[...]
-    grad[...] = times_table(merged, forward_back) * (1.0 - held * held)
+    merged_ref[...] = merged + table_times(rows_near[...], near)
     for copy in first_swap + second_swap:
         copy.wait_send()
 
 
-def store(resist, grad, resist_hbm, grad_hbm, sems):
-    copies = [
-        pltpu.make_async_copy(resist, resist_hbm, sems.at[0]),
-        pltpu.make_async_copy(grad, grad_hbm, sems.at[1]),
-    ]
-    for copy in copies:
+def finish(resist, merged, transmit, table, resist_hbm, grad_hbm, grad, sems):
+    copies = [pltpu.make_async_copy(resist, resist_hbm, sems.at[0])]
+    copies[0].start()
+    rows, columns = grad.shape
+    chunks = CHUNKS if columns % (128 * CHUNKS) == 0 else 1
+    high, low = split(merged[...])
+    left = jnp.concatenate([high, low], axis=0)
+    for at in range(chunks):
+        part = pl.ds(at * (columns // chunks), columns // chunks)
+        both = dot(left, table[0, :, part])
+        product = both[:rows] + (both[rows:] + dot(high, table[1, :, part]))
+        held = transmit[:, part]
+        grad[:, part] = product * (1.0 - held * held)
+        copy = pltpu.make_async_copy(grad.at[:, part], grad_hbm.at[:, part], sems.at[1 + at])
         copy.start()
+        copies.append(copy)
     for copy in copies:
         copy.wait()
 
@@ -320,17 +329,18 @@
     out = jax.ShapeDtypeStruct((strip_rows, columns), jnp.float32)
     held = pltpu.VMEM((strip_rows, columns), jnp.float32)
     in_vmem = pl.BlockSpec(memory_space=pltpu.VMEM)
-    resist, grad = pl.pallas_call(
+    merged = pltpu.VMEM((strip_rows, 2 * freq_cols), jnp.float32)
+    last = pltpu.VMEM(tables["forward_back"].shape, jnp.bfloat16)
+    results = pl.pallas_call(
         functools.partial(kernel, count, names),
-        out_shape=(held, held),
+        out_shape=(held, merged, held, last),
         in_specs=[pl.BlockSpec(memory_space=pltpu.SMEM)] + [anywhere] * (3 + len(names)),
-        out_specs=(in_vmem, in_vmem),
-        scratch_shapes=[pltpu.VMEM(t.shape, jnp.bfloat16) for t in tables.values()]
+        out_specs=(in_vmem,) * 4,
+        scratch_shapes=[pltpu.VMEM(tables[n].shape, jnp.bfloat16) for n in names if n != "forward_back"]
         + [
             pltpu.VMEM((strip_rows, columns), jnp.float32),
             pltpu.VMEM((strip_rows, columns), jnp.int32),
             pltpu.VMEM(kernel_spectra.shape, jnp.float32),
-            pltpu.VMEM((strip_rows, columns), jnp.float32),
             pltpu.VMEM((kernels // GROUP, 4 * freq_rows, GROUP * 2 * freq_cols), jnp.float32),
             pltpu.VMEM((2,) + spectrum, jnp.float32),
             pltpu.VMEM((2,) + spectrum, jnp.float32),
@@ -346,13 +356,17 @@
         name="litho_step",
     )(kernel_weights, mask_params, target, kernel_spectra, *[jnp.asarray(t) for t in tables.values()])
     return pl.pallas_call(
-        store,
+        finish,
         out_shape=(out, out),
-        in_specs=[in_vmem, in_vmem],
+        in_specs=[in_vmem] * 4,
         out_specs=(anywhere, anywhere),
-        scratch_shapes=[pltpu.SemaphoreType.DMA((2,))],
-        name="store_results",
-    )(*[pltpu.with_memory_space_constraint(x, pltpu.VMEM) for x in (resist, grad)])
+        scratch_shapes=[
+            pltpu.VMEM((strip_rows, columns), jnp.float32),
+            pltpu.SemaphoreType.DMA((1 + CHUNKS,)),
+        ],
+        compiler_params=pltpu.CompilerParams(vmem_limit_bytes=32 * 1024 * 1024),
+        name="finish_gradient",
+    )(*[pltpu.with_memory_space_constraint(x, pltpu.VMEM) for x in results])
 
 
 def solution(mesh):

time: 20.5 us -> 20.3 us (level)
    pallas_call x1, Pallas kernels: 18.7 us -> 18.4 us  [shards(): pl.pallas_call(functools.partial(kernel, count, names), out_shape=(held,...]
where the time goes in v10:
time: 20.3 us; the launch traced here: 20.1 us
  Pallas kernels  19.5 us (96%)
  between operations  0.64 us (3%)
    pallas_call x1, Pallas kernels, shards(): pl.pallas_call(functools.partial(kernel, count, names), out_shape=(held,...  18.4 us
    pallas_call x1, Pallas kernels, shards(): pl.pallas_call(finish, out_shape=(out, out), in_specs=[in_vmem] * 4, out_...  1.12 us

profile of v10, /device:TPU:0, one launch (start us, length us, event | category | flops | bytes accessed | tf_op | source)
XLA Modules:
  0.0 20.1 jit_solution(4229849833655072947)
XLA Ops:
  0.6 18.4 %litho_step.1 = (f32[128,1024]{1,0:T(8,128)S(1)}, f32[128,256]{1,0:T(8,128)S(1)}, f32[128,1024]{1,0:T(8,128)S(1)}, bf16[2,256,1024]{2,1,0:T(8,128)(2,1)S(1)}) custom-call(f32[16]{0:T(128)} %weights_ref.1, f32[128,1024]{1,0:T(8,128)} %mask_hbm.1, s32[128,1024]{1,0:T(8,128)} %target_hbm.1, f32[2,16,32,128]{3,2,1,0:T(8,128)} %spectra_hbm.1, ...), custom_call_target="tpu_custom_call" | custom-call | tf_op jit(solution)/shard_map/litho_step/pallas_call | solution.py:334
  19.0 1.1 %finish_gradient.1 = (f32[128,1024]{1,0:T(8,128)}, f32[128,1024]{1,0:T(8,128)}) custom-call(f32[128,1024]{1,0:T(8,128)S(1)} %get-tuple-element.6.resist, f32[128,256]{1,0:T(8,128)S(1)} %get-tuple-element.7.merged, f32[128,1024]{1,0:T(8,128)S(1)} %get-tuple-element.8.transmit, bf16[2,256,1024]{2,1,0:T(8,128)(2,1)S(1)} %get-tuple-element.9.table), custom_call_target="tpu_custom_call" | custom-call | tf_op jit(solution)/shard_map/finish_gradient/pallas_call | solution.py:358

commit v11 on v10

--- a/solution.py
+++ b/solution.py
@@ -14,6 +14,7 @@
 STEEPNESS = 8.0
 THRESHOLD = 0.35
 GROUP = 4
+BATCH = 8
 CHUNKS = 4
 MESH = pl.DeviceIdType.MESH
 
@@ -241,17 +242,20 @@
 
     coarse = fields.shape[1] // 2
     width = fields.shape[2] // GROUP
-    blocks = []
-    for k in range(kernels):
-        real = spectra[0, k] * spec_real - spectra[1, k] * spec_imag
-        imag = spectra[0, k] * spec_imag + spectra[1, k] * spec_real
-        blocks.append(jnp.concatenate([real, imag], axis=1))
-    across = times_long(jnp.concatenate(blocks, axis=0), inverse[...])
+    across = []
+    for first in range(0, kernels, BATCH):
+        blocks = []
+        for k in range(first, min(first + BATCH, kernels)):
+            real = spectra[0, k] * spec_real - spectra[1, k] * spec_imag
+            imag = spectra[0, k] * spec_imag + spectra[1, k] * spec_real
+            blocks.append(jnp.concatenate([real, imag], axis=1))
+        across.append(times_long(jnp.concatenate(blocks, axis=0), inverse[...]))
     power = None
     for group in range(fields.shape[0]):
         blocks = []
         for k in range(group * GROUP, (group + 1) * GROUP):
-            part = across[k * freq_rows : (k + 1) * freq_rows]
+            at = (k % BATCH) * freq_rows
+            part = across[k // BATCH][at : at + freq_rows]
             blocks.append(jnp.concatenate([part[:, :width], part[:, width:]], axis=0))
         field = table_times(rows_out[...], jnp.concatenate(blocks, axis=1))
         fields[group] = field
@@ -261,7 +265,7 @@
             power = term if power is None else power + term
 
     intensity = table_times(table("up_rows")[...], times_table(power, table("up_cols")))
-    image = jax.nn.sigmoid(STEEPNESS * (intensity - THRESHOLD))
+    image = 0.5 + 0.5 * jnp.tanh((0.5 * STEEPNESS) * (intensity - THRESHOLD))
     resist[...] = image
     loads["target"].wait()
     slopes = (4.0 * STEEPNESS) * (image - target[...].astype(jnp.float32)) * image * (1.0 - image)
@@ -276,10 +280,14 @@
         for place in range(GROUP):
             piece = part[:, place * width : (place + 1) * width]
             blocks.append(jnp.concatenate([piece[:freq_rows], piece[freq_rows:]], axis=1))
-    across = times_long(jnp.concatenate(blocks, axis=0), inverse_back[...])
+    across = [
+        times_long(jnp.concatenate(blocks[first : first + BATCH], axis=0), inverse_back[...])
+        for first in range(0, kernels, BATCH)
+    ]
     grad_real = grad_imag = None
     for k in range(kernels):
-        part = across[k * freq_rows : (k + 1) * freq_rows]
+        at = (k % BATCH) * freq_rows
+        part = across[k // BATCH][at : at + freq_rows]
         real, imag = part[:, :freq_cols], part[:, freq_cols:]
         term_real = real * spectra[0, k] + imag * spectra[1, k]
         term_imag = imag * spectra[0, k] - real * spectra[1, k]

time: 20.3 us -> 19.7 us (0.970)
  Pallas kernels: 19.5 us -> 18.9 us
    pallas_call x1, Pallas kernels: 18.4 us -> 17.7 us  [shards(): pl.pallas_call(functools.partial(kernel, count, names), out_shape=(held,...]
where the time goes in v11:
time: 19.7 us; the launch traced here: 19.5 us
  Pallas kernels  18.9 us (96%)
  between operations  0.64 us (3%)
    pallas_call x1, Pallas kernels, shards(): pl.pallas_call(functools.partial(kernel, count, names), out_shape=(held,...  17.7 us
    pallas_call x1, Pallas kernels, shards(): pl.pallas_call(finish, out_shape=(out, out), in_specs=[in_vmem] * 4, out_...  1.12 us

profile of v11, /device:TPU:0, one launch (start us, length us, event | category | flops | bytes accessed | tf_op | source)
XLA Modules:
  0.0 19.5 jit_solution(9835793202325979993)
XLA Ops:
  0.6 17.7 %litho_step.1 = (f32[128,1024]{1,0:T(8,128)S(1)}, f32[128,256]{1,0:T(8,128)S(1)}, f32[128,1024]{1,0:T(8,128)S(1)}, bf16[2,256,1024]{2,1,0:T(8,128)(2,1)S(1)}) custom-call(f32[16]{0:T(128)} %weights_ref.1, f32[128,1024]{1,0:T(8,128)} %mask_hbm.1, s32[128,1024]{1,0:T(8,128)} %target_hbm.1, f32[2,16,32,128]{3,2,1,0:T(8,128)} %spectra_hbm.1, ...), custom_call_target="tpu_custom_call" | custom-call | tf_op jit(solution)/shard_map/litho_step/pallas_call | solution.py:342
  18.4 1.1 %finish_gradient.1 = (f32[128,1024]{1,0:T(8,128)}, f32[128,1024]{1,0:T(8,128)}) custom-call(f32[128,1024]{1,0:T(8,128)S(1)} %get-tuple-element.6.resist, f32[128,256]{1,0:T(8,128)S(1)} %get-tuple-element.7.merged, f32[128,1024]{1,0:T(8,128)S(1)} %get-tuple-element.8.transmit, bf16[2,256,1024]{2,1,0:T(8,128)(2,1)S(1)} %get-tuple-element.9.table), custom_call_target="tpu_custom_call" | custom-call | tf_op jit(solution)/shard_map/finish_gradient/pallas_call | solution.py:366
